TPU v7x, 32 devices: a whole 2x2x4 slice. The times are simulated.
32 devices in a mesh: groups: 2 (over y), ep: 8 (over z, core), hg: 2 (over x).
Axes of the slice: x: 2, y: 2, z: 4, core: 2. Of those that a mesh axis runs over, the one named last changes fastest.
Arguments:
- queries: bfloat16 [3, 128, 64, 128], P(None, ('groups', 'ep'), 'hg'), parts along dimension 1, may hold values from -12 to 12
- key_cache: bfloat16 [3, 128, 4, 96, 128], P(None, ('groups', 'ep'), 'hg'), parts along dimension 1, may hold values from -5 to 5
- value_cache: bfloat16 [3, 128, 4, 96, 128], P(None, ('groups', 'ep'), 'hg'), parts along dimension 1, may hold values from -6 to 6
- lengths: int32 [3, 128], P(None, ('groups', 'ep')), parts along dimension 1, may hold values from 2 to 96, as said below
- residual: bfloat16 [3, 128, 4096], P(None, ('groups', 'ep')), parts along dimension 1, may hold values from -6 to 6
- out_weight: bfloat16 [8192, 4096], P('hg', 'ep'), may hold values from -0.0625 to 0.0625
- norm_gain: float32 [4096], replicated, may hold values from 0.1 to 1.9
- routes: int32 [3, 128, 8], P(None, ('groups', 'ep')), parts along dimension 1, may hold values from 0 to 15, all different within a row; in each aligned block of 8 rows (0 to 7, 8 to 15, ..., all dimensions but the last counted through in order) at most 8 rows name the same one
- route_probs: float32 [3, 128, 8], P(None, ('groups', 'ep')), parts along dimension 1, may hold values from 0.05 to 1
- gate_weight: bfloat16 [16, 4096, 768], P('ep', None, 'hg'), may hold values from -0.09375 to 0.09375
- up_weight: bfloat16 [16, 4096, 768], P('ep', None, 'hg'), may hold values from -0.09375 to 0.09375
- down_weight: bfloat16 [16, 768, 4096], P('ep', 'hg'), may hold values from -0.21875 to 0.21875
Outputs:
- layer_out: bfloat16 [3, 128, 4096], P(None, ('groups', 'ep'), 'hg'), parts along dimension 1
There are 2 independent parts, one for each index of `groups`. A program takes and returns all parts, laid end to end along the dimension named above; an argument that names none is the same for every part. Nothing has to cross between parts.
Inputs may be any that keep to these rules, and one draw needn't show every extreme that they name: `routes`: in the 8 rows of one micro-batch on one index of ep (aligned blocks), no expert is named more than 8 times, a bound that some block reaches; a row names 8 different experts. `lengths`: some row of every draw has all 96 slots live.
All inputs are finite; a program needn't handle non-finite values.
Results may differ from a plain program's by a relative error of at most 0.0075.
Values may be sent and summed in bfloat16 or wider, within the bound.
A program may use at most 128 MiB of HBM per device.

v0:
```python
import math

import jax
import jax.numpy as jnp
from jax import lax
from jax.sharding import PartitionSpec as P


def attention_block(queries, key_cache, value_cache, lengths):
    batch_size, row_count, head_count, head_size = queries.shape
    kv_count = key_cache.shape[2]
    key_span = key_cache.shape[3]
    grouped = queries.reshape(batch_size, row_count, kv_count, head_count // kv_count, head_size)
    scores = jnp.einsum(
        "brgjd,brgtd->brgjt", grouped, key_cache, preferred_element_type=jnp.float32
    ) / math.sqrt(head_size)
    live_mask = lax.broadcasted_iota(jnp.int32, (1, 1, key_span), 2) < lengths[:, :, None]
    scores = jnp.where(live_mask[:, :, None, None, :], scores, -1e30)
    weights = jax.nn.softmax(scores, axis=-1).astype(jnp.bfloat16)
    mixed_heads = jnp.einsum(
        "brgjt,brgtd->brgjd", weights, value_cache, preferred_element_type=jnp.float32
    )
    return mixed_heads.astype(jnp.bfloat16).reshape(batch_size, row_count, head_count * head_size)


def shards(
    queries,
    key_cache,
    value_cache,
    lengths,
    residual,
    out_weight,
    norm_gain,
    routes,
    route_probs,
    gate_weight,
    up_weight,
    down_weight,
):
    ep_count = lax.axis_size("ep")
    hg_count = lax.axis_size("hg")
    row_count = queries.shape[1]
    top_count = routes.shape[2]
    model_width = residual.shape[2]
    expert_count = gate_weight.shape[0] * ep_count
    capacity = min(row_count, max(2, 2 * row_count * top_count // expert_count))
    slot_count = expert_count * capacity
    share_width = model_width // hg_count
    column_start = lax.axis_index("hg") * share_width
    results = []
    for batch_index in range(queries.shape[0]):
        upper = batch_index + 1
        queries_part = queries[batch_index:upper]
        probs_part = route_probs[batch_index:upper]
        batch_size = queries_part.shape[0]
        attended = attention_block(
            queries_part,
            key_cache[batch_index:upper],
            value_cache[batch_index:upper],
            lengths[batch_index:upper],
        )
        partial_value = jnp.einsum(
            "bnk,kc->bnc",
            lax.all_gather(attended, "ep", axis=1, tiled=True),
            out_weight,
            preferred_element_type=jnp.float32,
        )
        own_rows = lax.all_to_all(partial_value, "ep", split_axis=1, concat_axis=2, tiled=True)
        projected = lax.psum(own_rows, "hg")
        hidden = residual[batch_index:upper].astype(jnp.float32) + projected
        scale = lax.rsqrt(jnp.mean(hidden * hidden, axis=-1, keepdims=True) + 1e-06)
        payload = (hidden * scale * norm_gain).astype(jnp.bfloat16)
        flat_routes = routes[batch_index:upper].reshape(batch_size, row_count * top_count)
        onehot = (
            flat_routes[:, :, None] == lax.broadcasted_iota(jnp.int32, (1, 1, expert_count), 2)
        ).astype(jnp.int32)
        before = jnp.cumsum(onehot, axis=1) - onehot
        slot_index = jnp.sum(before * onehot, axis=-1)
        target = flat_routes * capacity + slot_index
        placed = (
            target[:, :, None] == lax.broadcasted_iota(jnp.int32, (1, 1, slot_count), 2)
        ).astype(jnp.bfloat16)
        selector = jnp.sum(placed.reshape(batch_size, row_count, top_count, slot_count), axis=2)
        buffer = jnp.einsum(
            "bre,brd->bed", selector, payload, preferred_element_type=jnp.float32
        ).astype(jnp.bfloat16)
        buffer = buffer.reshape(
            batch_size, ep_count, expert_count // ep_count, capacity, payload.shape[2]
        )
        received = lax.all_to_all(buffer, "ep", split_axis=1, concat_axis=1, tiled=True)
        gate_value = jnp.einsum(
            "bsjcd,jdh->bsjch", received, gate_weight, preferred_element_type=jnp.float32
        )
        up_value = jnp.einsum(
            "bsjcd,jdh->bsjch", received, up_weight, preferred_element_type=jnp.float32
        )
        activation = (jax.nn.silu(gate_value) * up_value).astype(jnp.bfloat16)
        partial_out = jnp.einsum(
            "bsjch,jhd->bsjcd", activation, down_weight, preferred_element_type=jnp.float32
        )
        summed = lax.psum_scatter(partial_out, "hg", scatter_dimension=4, tiled=True).astype(
            jnp.bfloat16
        )
        returned = lax.all_to_all(summed, "ep", split_axis=1, concat_axis=1, tiled=True)
        returned = returned.reshape(batch_size, slot_count, share_width)
        picked = jnp.einsum("bae,bed->bad", placed, returned, preferred_element_type=jnp.float32)
        picked = picked.reshape(batch_size, row_count, top_count, share_width)
        gate_share = probs_part / jnp.sum(probs_part, axis=-1, keepdims=True)
        expert_mix = jnp.sum(gate_share[..., None] * picked, axis=2)
        hidden_share = lax.dynamic_slice_in_dim(hidden, column_start, share_width, 2)
        results.append((hidden_share + expert_mix).astype(jnp.bfloat16))
    return jnp.concatenate(results, axis=0)


def solution(mesh):
    return jax.shard_map(
        shards,
        mesh=mesh,
        in_specs=(
            P(None, ("groups", "ep"), "hg", None),
            P(None, ("groups", "ep"), "hg", None, None),
            P(None, ("groups", "ep"), "hg", None, None),
            P(None, ("groups", "ep")),
            P(None, ("groups", "ep"), None),
            P("hg", "ep"),
            P(),
            P(None, ("groups", "ep"), None),
            P(None, ("groups", "ep"), None),
            P("ep", None, "hg"),
            P("ep", None, "hg"),
            P("ep", "hg", None),
        ),
        out_specs=P(None, ("groups", "ep"), "hg"),
        check_vma=False,
    )
```

profile of v0, /device:TPU:0, one launch (start us, length us, event | category | flops | bytes accessed | tf_op | source)
XLA Modules:
  0.0 317.6 jit_solution(10125256331224097884)
XLA Ops:
  8.5 1.3 fusion.72
  10.0 1.5 convolution_convert_fusion.3
  11.6 16.6 %all_gather.11 = bf16[1,64,4096]{2,1,0:T(8,128)(2,1)S(1)} all-gather(bf16[1,8,4096]{2,1,0:T(8,128)(2,1)S(1)} %reshape.970), channel_id=1, replica_groups=mesh['groups'=2,'ep'=8,'hg'=2] {'ep'}, dimensions={1}, use_global_device_ids=true | all-gather | bytes 589824 | tf_op jit(solution)/shard_map/all_gather | solution.py:64
  28.2 3.0 convolution_bitcast_fusion
  32.0 4.6 %all-to-all-start.6 = ((f32[1,64,512]{2,0,1:T(1,128)}), f32[1,64,512]{2,0,1:T(1,128)S(1)}, u32[]{:S(2)}, u32[]{:S(2)}) async-start(f32[1,64,512]{2,0,1:T(1,128)} %copy.47), calls=%async_computation.8 | async-start | bytes 262144 | tf_op jit(solution)/shard_map/all_to_all | solution.py:68
  37.8 15.4 %all_gather.10 = bf16[1,64,4096]{2,1,0:T(8,128)(2,1)S(1)} all-gather(bf16[1,8,4096]{2,1,0:T(8,128)(2,1)S(1)} %reshape.959), channel_id=1, replica_groups=mesh['groups'=2,'ep'=8,'hg'=2] {'ep'}, dimensions={1}, use_global_device_ids=true | all-gather | bytes 589824 | tf_op jit(solution)/shard_map/all_gather | solution.py:64
  53.2 3.1 convolution_bitcast_fusion.1
  58.2 14.8 %all_gather.9 = bf16[1,64,4096]{2,1,0:T(8,128)(2,1)S(1)} all-gather(bf16[1,8,4096]{2,1,0:T(8,128)(2,1)S(1)} %reshape.948), channel_id=1, replica_groups=mesh['groups'=2,'ep'=8,'hg'=2] {'ep'}, dimensions={1}, use_global_device_ids=true | all-gather | bytes 589824 | tf_op jit(solution)/shard_map/all_gather | solution.py:64
  72.9 3.0 convolution_bitcast_fusion.2
  76.0 4.8 %all-to-all-start.3 = ((f32[1,64,512]{2,0,1:T(1,128)}), f32[1,64,512]{2,0,1:T(1,128)S(1)}, u32[]{:S(2)}, u32[]{:S(2)}) async-start(f32[1,64,512]{2,0,1:T(1,128)} %copy.42), calls=%async_computation.4 | async-start | bytes 262144 | tf_op jit(solution)/shard_map/all_to_all | solution.py:68
  81.9 5.7 %all-to-all-done.3 = f32[1,64,512]{2,0,1:T(1,128)S(1)} async-done(((f32[1,64,512]{2,0,1:T(1,128)}), f32[1,64,512]{2,0,1:T(1,128)S(1)}, u32[]{:S(2)}, u32[]{:S(2)}) %all-to-all-start.3) | async-done | bytes 131104 | tf_op jit(solution)/shard_map/all_to_all | solution.py:68
  87.6 3.4 %all-to-all-start = ((f32[1,64,512]{2,0,1:T(1,128)}), f32[1,64,512]{2,0,1:T(1,128)S(1)}, u32[]{:S(2)}, u32[]{:S(2)}) async-start(f32[1,64,512]{2,0,1:T(1,128)} %copy.37), calls=%async_computation | async-start | bytes 262144 | tf_op jit(solution)/shard_map/all_to_all | solution.py:68
  93.1 4.6 %all-to-all-done = f32[1,64,512]{2,0,1:T(1,128)S(1)} async-done(((f32[1,64,512]{2,0,1:T(1,128)}), f32[1,64,512]{2,0,1:T(1,128)S(1)}, u32[]{:S(2)}, u32[]{:S(2)}) %all-to-all-start) | async-done | bytes 131104 | tf_op jit(solution)/shard_map/all_to_all | solution.py:68
  99.0 24.7 %all-reduce.3.cloned.1.call-done = (f32[1,8,4096]{2,1,0:T(8,128)}, f32[1,8,4096]{2,1,0:T(8,128)}, f32[1,8,4096]{2,1,0:T(8,128)}) async-done(((f32[1,8,4096]{2,1,0:T(8,128)}, f32[1,8,4096]{2,1,0:T(8,128)}, f32[1,8,4096]{2,1,0:T(8,128)}), (f32[1,8,4096]{2,1,0:T(8,128)}, f32[1,8,4096]{2,1,0:T(8,128)}, f32[1,8,4096]{2,1,0:T(8,128)})) %all-reduce.3.cloned.1.call-update) | async-done | bytes 393232 | tf_op jit(solution)/shard_map/psum | solution.py:69
  125.4 31.0 %all_to_all.84 = bf16[1,8,2,8,4096]{4,3,2,0,1:T(8,128)(2,1)S(1)} all-to-all(bf16[1,8,2,8,4096]{4,3,2,0,1:T(8,128)(2,1)S(1)} %bitcast.318), channel_id=1, replica_groups=mesh['groups'=2,'ep'=8,'hg'=2] {'ep'}, dimensions={1} | all-to-all | bytes 2097152 | tf_op jit(solution)/shard_map/all_to_all | solution.py:90
  156.4 3.8 %fusion.39 = f32[1,8,2,8,384]{4,3,1,2,0:T(8,128)S(1)} fusion(bf16[2,4096,384]{2,1,0:T(8,128)(2,1)} %param.21, bf16[1,8,2,8,4096]{4,3,2,0,1:T(8,128)(2,1)S(1)} %all_to_all.84), kind=kOutput, calls=%fused_computation.35 | convolution fusion | flops 402653184 | bytes 7536640 | tf_op jit(solution)/shard_map/bsjcd,jdh->bsjch/dot_general | solution.py:91
  160.3 8.1 %fusion.27 = f32[1,8,2,8,4096]{4,3,1,2,0:T(8,128)} fusion(bf16[2,384,4096]{2,1,0:T(8,128)(2,1)} %param.23, bf16[2,4096,384]{2,1,0:T(8,128)(2,1)} %param.22, bf16[1,8,2,8,4096]{4,3,2,0,1:T(8,128)(2,1)S(1)} %all_to_all.84, f32[1,8,2,8,384]{4,3,1,2,0:T(8,128)S(1)} %fusion.39), kind=kOutput, calls=%fused_computation.23 | convolution fusion | flops 805601280 | bytes 15925248 | tf_op jit(solution)/shard_map/bsjch,jhd->bsjcd/dot_general | solution.py:98
  168.9 29.0 %all_to_all.85 = bf16[1,8,2,8,4096]{4,3,2,0,1:T(8,128)(2,1)S(1)} all-to-all(bf16[1,8,2,8,4096]{4,3,2,0,1:T(8,128)(2,1)S(1)} %bitcast.319), channel_id=1, replica_groups=mesh['groups'=2,'ep'=8,'hg'=2] {'ep'}, dimensions={1} | all-to-all | bytes 2097152 | tf_op jit(solution)/shard_map/all_to_all | solution.py:90
  197.9 3.9 %fusion.36 = f32[1,8,2,8,384]{4,3,1,2,0:T(8,128)S(1)} fusion(bf16[2,4096,384]{2,1,0:T(8,128)(2,1)} %param.21, bf16[1,8,2,8,4096]{4,3,2,0,1:T(8,128)(2,1)S(1)} %all_to_all.85), kind=kOutput, calls=%fused_computation.34 | convolution fusion | flops 402653184 | bytes 7536640 | tf_op jit(solution)/shard_map/bsjcd,jdh->bsjch/dot_general | solution.py:91
  201.8 8.0 %fusion.24 = f32[1,8,2,8,4096]{4,3,1,2,0:T(8,128)} fusion(bf16[2,384,4096]{2,1,0:T(8,128)(2,1)} %param.23, bf16[2,4096,384]{2,1,0:T(8,128)(2,1)} %param.22, bf16[1,8,2,8,4096]{4,3,2,0,1:T(8,128)(2,1)S(1)} %all_to_all.85, f32[1,8,2,8,384]{4,3,1,2,0:T(8,128)S(1)} %fusion.36), kind=kOutput, calls=%fused_computation.22 | convolution fusion | flops 805601280 | bytes 15925248 | tf_op jit(solution)/shard_map/bsjch,jhd->bsjcd/dot_general | solution.py:98
  210.5 29.0 %all_to_all.86 = bf16[1,8,2,8,4096]{4,3,2,0,1:T(8,128)(2,1)S(1)} all-to-all(bf16[1,8,2,8,4096]{4,3,2,0,1:T(8,128)(2,1)S(1)} %bitcast.320), channel_id=1, replica_groups=mesh['groups'=2,'ep'=8,'hg'=2] {'ep'}, dimensions={1} | all-to-all | bytes 2097152 | tf_op jit(solution)/shard_map/all_to_all | solution.py:90
  239.5 3.9 %fusion.33 = f32[1,8,2,8,384]{4,3,1,2,0:T(8,128)S(1)} fusion(bf16[2,4096,384]{2,1,0:T(8,128)(2,1)} %param.21, bf16[1,8,2,8,4096]{4,3,2,0,1:T(8,128)(2,1)S(1)} %all_to_all.86), kind=kOutput, calls=%fused_computation.33 | convolution fusion | flops 402653184 | bytes 7536640 | tf_op jit(solution)/shard_map/bsjcd,jdh->bsjch/dot_general | solution.py:91
  243.4 8.1 %fusion.21 = f32[1,8,2,8,4096]{4,3,1,2,0:T(8,128)} fusion(bf16[2,384,4096]{2,1,0:T(8,128)(2,1)} %param.23, bf16[2,4096,384]{2,1,0:T(8,128)(2,1)} %param.22, bf16[1,8,2,8,4096]{4,3,2,0,1:T(8,128)(2,1)S(1)} %all_to_all.86, f32[1,8,2,8,384]{4,3,1,2,0:T(8,128)S(1)} %fusion.33), kind=kOutput, calls=%fused_computation.21 | convolution fusion | flops 805601280 | bytes 15925248 | tf_op jit(solution)/shard_map/bsjch,jhd->bsjcd/dot_general | solution.py:98
  251.6 1.3 convert_element_type.199
  253.7 3.5 %all-to-all-start.8 = ((bf16[1,8,2,8,2048]{4,3,2,0,1:T(8,128)(2,1)}), bf16[1,8,2,8,2048]{4,3,2,0,1:T(8,128)(2,1)S(1)}, u32[]{:S(2)}, u32[]{:S(2)}) async-start(bf16[1,8,2,8,2048]{4,3,2,0,1:T(8,128)(2,1)} %copy.51), calls=%async_computation.11 | async-start | bytes 1048576 | tf_op jit(solution)/shard_map/all_to_all | solution.py:104
  257.3 1.3 convert_element_type.189
  259.4 13.1 %all-to-all-done.8 = bf16[1,8,2,8,2048]{4,3,2,0,1:T(8,128)(2,1)S(1)} async-done(((bf16[1,8,2,8,2048]{4,3,2,0,1:T(8,128)(2,1)}), bf16[1,8,2,8,2048]{4,3,2,0,1:T(8,128)(2,1)S(1)}, u32[]{:S(2)}, u32[]{:S(2)}) %all-to-all-start.8) | async-done | bytes 524320 | tf_op jit(solution)/shard_map/all_to_all | solution.py:104
  272.5 3.5 %all-to-all-start.5 = ((bf16[1,8,2,8,2048]{4,3,2,0,1:T(8,128)(2,1)}), bf16[1,8,2,8,2048]{4,3,2,0,1:T(8,128)(2,1)S(1)}, u32[]{:S(2)}, u32[]{:S(2)}) async-start(bf16[1,8,2,8,2048]{4,3,2,0,1:T(8,128)(2,1)} %copy.46), calls=%async_computation.7 | async-start | bytes 1048576 | tf_op jit(solution)/shard_map/all_to_all | solution.py:104
  276.3 5.2 %reduce-scatter.4.cloned.1.call-done = f32[1,8,2,8,2048]{4,3,1,2,0:T(8,128)} async-done(((f32[1,8,2,8,4096]{4,3,1,2,0:T(8,128)}), f32[1,8,2,8,2048]{4,3,1,2,0:T(8,128)}) %reduce-scatter.4.cloned.1.call-update) | async-done | bytes 1048592 | tf_op jit(solution)/shard_map/reduce_scatter | solution.py:101
  284.0 7.3 %all-to-all-done.5 = bf16[1,8,2,8,2048]{4,3,2,0,1:T(8,128)(2,1)S(1)} async-done(((bf16[1,8,2,8,2048]{4,3,2,0,1:T(8,128)(2,1)}), bf16[1,8,2,8,2048]{4,3,2,0,1:T(8,128)(2,1)S(1)}, u32[]{:S(2)}, u32[]{:S(2)}) %all-to-all-start.5) | async-done | bytes 524320 | tf_op jit(solution)/shard_map/all_to_all | solution.py:104
  291.3 3.5 %all-to-all-start.2 = ((bf16[1,8,2,8,2048]{4,3,2,0,1:T(8,128)(2,1)}), bf16[1,8,2,8,2048]{4,3,2,0,1:T(8,128)(2,1)S(1)}, u32[]{:S(2)}, u32[]{:S(2)}) async-start(bf16[1,8,2,8,2048]{4,3,2,0,1:T(8,128)(2,1)} %copy.41), calls=%async_computation.3 | async-start | bytes 1048576 | tf_op jit(solution)/shard_map/all_to_all | solution.py:104
  295.2 14.9 %all-to-all-done.2 = bf16[1,8,2,8,2048]{4,3,2,0,1:T(8,128)(2,1)S(1)} async-done(((bf16[1,8,2,8,2048]{4,3,2,0,1:T(8,128)(2,1)}), bf16[1,8,2,8,2048]{4,3,2,0,1:T(8,128)(2,1)S(1)}, u32[]{:S(2)}, u32[]{:S(2)}) %all-to-all-start.2) | async-done | bytes 524320 | tf_op jit(solution)/shard_map/all_to_all | solution.py:104
  (85 shorter events, 19.3 us)
Async XLA Ops:
  6.5 30.2 %copy-start = (bf16[3,8,2,96,128]{4,3,2,1,0:T(8,128)(2,1)S(1)}, bf16[3,8,2,96,128]{4,3,2,1,0:T(8,128)(2,1)}, u32[]{:S(2)}) copy-start(bf16[3,8,2,96,128]{4,3,2,1,0:T(8,128)(2,1)} %param.13) | copy-start | bytes 3538948
  6.5 30.7 %copy-start.5 = (bf16[3,8,2,96,128]{4,3,2,1,0:T(8,128)(2,1)S(1)}, bf16[3,8,2,96,128]{4,3,2,1,0:T(8,128)(2,1)}, u32[]{:S(2)}) copy-start(bf16[3,8,2,96,128]{4,3,2,1,0:T(8,128)(2,1)} %param.14) | copy-start | bytes 3538948
  6.5 30.1 %copy-start.4 = (s32[3,8,8]{2,1,0:T(8,128)S(1)}, s32[3,8,8]{2,1,0:T(8,128)}, u32[]{:S(2)}) copy-start(s32[3,8,8]{2,1,0:T(8,128)} %param.19) | copy-start | bytes 2308
  32.0 44.0 %all-to-all-start.6 = ((f32[1,64,512]{2,0,1:T(1,128)}), f32[1,64,512]{2,0,1:T(1,128)S(1)}, u32[]{:S(2)}, u32[]{:S(2)}) async-start(f32[1,64,512]{2,0,1:T(1,128)} %copy.47), calls=%async_computation.8 | async-start | bytes 262144 | tf_op jit(solution)/shard_map/all_to_all | solution.py:68
  53.2 70.5 %copy-start.1 = (bf16[3,8,4096]{2,1,0:T(8,128)(2,1)S(1)}, bf16[3,8,4096]{2,1,0:T(8,128)(2,1)}, u32[]{:S(2)}) copy-start(bf16[3,8,4096]{2,1,0:T(8,128)(2,1)} %param.16) | copy-start | bytes 589828
  56.2 68.7 %copy-start.2 = (f32[4096]{0:T(1024)S(1)}, f32[4096]{0:T(1024)}, u32[]{:S(2)}) copy-start(f32[4096]{0:T(1024)} %param.18) | copy-start | bytes 49156
  76.0 11.6 %all-to-all-start.3 = ((f32[1,64,512]{2,0,1:T(1,128)}), f32[1,64,512]{2,0,1:T(1,128)S(1)}, u32[]{:S(2)}, u32[]{:S(2)}) async-start(f32[1,64,512]{2,0,1:T(1,128)} %copy.42), calls=%async_computation.4 | async-start | bytes 262144 | tf_op jit(solution)/shard_map/all_to_all | solution.py:68
  87.6 10.1 %all-to-all-start = ((f32[1,64,512]{2,0,1:T(1,128)}), f32[1,64,512]{2,0,1:T(1,128)S(1)}, u32[]{:S(2)}, u32[]{:S(2)}) async-start(f32[1,64,512]{2,0,1:T(1,128)} %copy.37), calls=%async_computation | async-start | bytes 262144 | tf_op jit(solution)/shard_map/all_to_all | solution.py:68
  91.0 32.7 %all-reduce.3.cloned.1.call-start = ((), (), s32[]{:S(2)}) async-start(), calls=%async_computation.15 | async-start | bytes 786432 | tf_op jit(solution)/shard_map/psum | solution.py:69
  98.4 153.2 %reduce-scatter.8.cloned.1.call-start = ((), (), s32[]{:S(2)}) async-start(), calls=%async_computation.14 | async-start | bytes 3145728 | tf_op jit(solution)/shard_map/reduce_scatter | solution.py:101
  168.4 88.9 %reduce-scatter.6.cloned.1.call-start = ((), (), s32[]{:S(2)}) async-start(), calls=%async_computation.13 | async-start | bytes 3145728 | tf_op jit(solution)/shard_map/reduce_scatter | solution.py:101
  209.9 71.6 %reduce-scatter.4.cloned.1.call-start = ((), (), s32[]{:S(2)}) async-start(), calls=%async_computation.12 | async-start | bytes 3145728 | tf_op jit(solution)/shard_map/reduce_scatter | solution.py:101
  251.5 24.5 %copy-start.3 = (f32[3,8,8]{2,1,0:T(8,128)S(1)}, f32[3,8,8]{2,1,0:T(8,128)}, u32[]{:S(2)}) copy-start(f32[3,8,8]{2,1,0:T(8,128)} %param.20) | copy-start | bytes 2308
  253.7 18.8 %all-to-all-start.8 = ((bf16[1,8,2,8,2048]{4,3,2,0,1:T(8,128)(2,1)}), bf16[1,8,2,8,2048]{4,3,2,0,1:T(8,128)(2,1)S(1)}, u32[]{:S(2)}, u32[]{:S(2)}) async-start(bf16[1,8,2,8,2048]{4,3,2,0,1:T(8,128)(2,1)} %copy.51), calls=%async_computation.11 | async-start | bytes 1048576 | tf_op jit(solution)/shard_map/all_to_all | solution.py:104
  272.5 18.8 %all-to-all-start.5 = ((bf16[1,8,2,8,2048]{4,3,2,0,1:T(8,128)(2,1)}), bf16[1,8,2,8,2048]{4,3,2,0,1:T(8,128)(2,1)S(1)}, u32[]{:S(2)}, u32[]{:S(2)}) async-start(bf16[1,8,2,8,2048]{4,3,2,0,1:T(8,128)(2,1)} %copy.46), calls=%async_computation.7 | async-start | bytes 1048576 | tf_op jit(solution)/shard_map/all_to_all | solution.py:104
  291.3 18.8 %all-to-all-start.2 = ((bf16[1,8,2,8,2048]{4,3,2,0,1:T(8,128)(2,1)}), bf16[1,8,2,8,2048]{4,3,2,0,1:T(8,128)(2,1)S(1)}, u32[]{:S(2)}, u32[]{:S(2)}) async-start(bf16[1,8,2,8,2048]{4,3,2,0,1:T(8,128)(2,1)} %copy.41), calls=%async_computation.3 | async-start | bytes 1048576 | tf_op jit(solution)/shard_map/all_to_all | solution.py:104
Sparse Core Ops, SparseCore 0:
  98.5 25.1 all-reduce.2
  168.5 29.7 reduce-scatter.7
  210.0 29.7 reduce-scatter.5
  251.7 29.7 reduce-scatter.3
where the time goes:
time: 319 us; the launch traced here: 318 us
  blocking collectives  136 us (43%)
  waiting for transfers between devices  75.6 us (24%)
  matrix products  51.8 us (16%)
  starting transfers between devices  23.5 us (7%)
  between operations  13.5 us (4%)
  local copies, waits for them, and re-layouts  9.37 us (3%)
  other arithmetic  8.09 us (3%)
    all_to_all x3, blocking collectives, shards(): lax.all_to_all(buffer, 'ep', split_axis=1, concat_axis=1, tiled=True)  89 us
    all_gather x3, blocking collectives, shards(): lax.all_gather(attended, 'ep', axis=1, tiled=True)  46.7 us
    all_to_all x3, waiting for transfers between devices, shards(): lax.all_to_all(summed, 'ep', split_axis=1, concat_axis=1, tiled=True)  35.3 us
    psum x1, waiting for transfers between devices, shards(): projected = lax.psum(own_rows, 'hg')  24.7 us
    dot_general x3, matrix products, shards(): jnp.einsum('bsjch,jhd->bsjcd', activation, down_weight, preferred_element...  24.2 us
    all_to_all x3, starting transfers between devices, shards(): lax.all_to_all(partial_value, 'ep', split_axis=1, concat_axis=2, tiled=True)  12.8 us
    dot_general x3, matrix products, shards(): jnp.einsum('bsjcd,jdh->bsjch', received, gate_weight, preferred_element_t...  11.6 us
    all_to_all x3, starting transfers between devices, shards(): lax.all_to_all(summed, 'ep', split_axis=1, concat_axis=1, tiled=True)  10.5 us
  transfers between devices with their start and end apart: 10, of which 7 were waited for; matrix products, arithmetic and copies ran while one was open for 14% of the time, Pallas kernels for 0%

commit v1 on v0

v1 whole, which is shorter than its diff:
```python
import functools
import math

import jax
import jax.numpy as jnp
from jax import lax
from jax.experimental import pallas as pl
from jax.experimental.pallas import tpu as pltpu
from jax.sharding import PartitionSpec as P

MESH = pl.DeviceIdType.MESH
F32 = jnp.float32
BF16 = jnp.bfloat16


def layer_kernel(
    dims,
    q_ref, k_ref, v_ref, len_ref, res_ref, gain_ref, routes_ref, probs_ref,
    wo_hbm, wg_hbm, wu_hbm, wd_hbm,
    out_ref,
    wo, wg, wu, wd, mixed, att, resb, wbuf, proj, hx_out, hx_in, hid,
    acc_g, acc_u, ssq, act, mine, d1_out, d1_in, d2_out, d2_in, d3_out, d3_in,
    w_sem, rs_send, rs_recv, sh_send, sh_recv, a_send, a_recv, hx_send, hx_recv,
    h_send, h_recv, d1_send, d1_recv, d2_send, d2_recv, d3_send, d3_recv,
):
    E, H, G, R, NC, NW, Q, QW, J = dims
    Z = E // 2
    ROWS = E * R
    D = res_ref.shape[1]
    CB = D // E
    DH = D // H
    me = lax.axis_index("ep")
    h = lax.axis_index("hg")
    z = me // 2
    c = me % 2
    partner = z * 2 + (1 - c)

    barrier = pltpu.get_barrier_semaphore()

    def greet_ep(i, _):
        pl.semaphore_signal(barrier, inc=1, device_id={"ep": (me + i) % E}, device_id_type=MESH)
        return 0

    def greet_hg(i, _):
        pl.semaphore_signal(barrier, inc=1, device_id={"hg": (h + i) % H}, device_id_type=MESH)
        return 0

    lax.fori_loop(1, E, greet_ep, 0)
    lax.fori_loop(1, H, greet_hg, 0)

    loads = [
        pltpu.make_async_copy(src, dst, w_sem.at[i])
        for i, (src, dst) in enumerate(((wo_hbm, wo), (wg_hbm, wg), (wu_hbm, wu), (wd_hbm, wd)))
    ]
    for load in loads:
        load.start()

    probs = probs_ref[...]
    share = probs / jnp.sum(probs, axis=-1, keepdims=True)
    routes = routes_ref[...]
    lanes = lax.broadcasted_iota(jnp.int32, (R, wbuf.shape[2]), 1)
    dense = jnp.zeros((R, wbuf.shape[2]), F32)
    for t in range(routes.shape[1]):
        dense = dense + jnp.where(lanes == routes[:, t : t + 1], share[:, t : t + 1], 0.0)
    wbuf[me] = dense

    pl.semaphore_wait(barrier, E - 1 + H - 1)

    def share_copy(dst):
        return pltpu.make_async_remote_copy(
            src_ref=wbuf.at[me], dst_ref=wbuf.at[me],
            send_sem=sh_send.at[dst], recv_sem=sh_recv.at[me],
            device_id={"ep": dst}, device_id_type=MESH,
        )

    def res_copy(dst):
        return pltpu.make_async_remote_copy(
            src_ref=res_ref.at[:, pl.ds(pl.multiple_of(dst * CB, CB), CB)], dst_ref=resb.at[me],
            send_sem=rs_send.at[dst], recv_sem=rs_recv.at[me],
            device_id={"ep": dst}, device_id_type=MESH,
        )

    def spread(i, _):
        dst = (me + i) % E
        res_copy(dst).start()
        share_copy(dst).start()
        return 0

    lax.fori_loop(1, E, spread, 0)
    resb[me] = res_ref[:, pl.ds(pl.multiple_of(me * CB, CB), CB)]

    def gather(place, send, recv, chunks, own_ready, process):
        def copy(k, block, way):
            target = (partner, me + 2, me - 2)[way]
            return pltpu.make_async_remote_copy(
                src_ref=place(k, block), dst_ref=place(k, block),
                send_sem=send.at[k, block, way], recv_sem=recv.at[k, block],
                device_id={"ep": target}, device_id_type=MESH,
            )

        def landed(k, block):
            pltpu.make_async_remote_copy(
                src_ref=place(k, block), dst_ref=place(k, block),
                send_sem=send.at[k, block, 0], recv_sem=recv.at[k, block],
                device_id={"ep": partner}, device_id_type=MESH,
            ).wait_recv()

        for k in range(chunks):
            own_ready(k)

            @pl.when(z < Z - 1)
            def _():
                copy(k, me, 1).start()

            @pl.when(z > 0)
            def _():
                copy(k, me, 2).start()

            copy(k, me, 0).start()

        def step(s, _):
            for k in range(chunks):

                @pl.when(z - s >= 0)
                def _():
                    block = me - 2 * s
                    landed(k, block)

                    @pl.when(z < Z - 1)
                    def _():
                        copy(k, block, 1).start()

                    copy(k, block, 0).start()

                @pl.when(z + s < Z)
                def _():
                    block = me + 2 * s
                    landed(k, block)

                    @pl.when(z > 0)
                    def _():
                        copy(k, block, 2).start()

                    copy(k, block, 0).start()

            before = s - 1

            @pl.when(z - before >= 0)
            def _():
                for k in range(chunks):
                    landed(k, partner - 2 * before)
                process(z - before)

            @pl.when((before > 0) & (z + before < Z))
            def _():
                for k in range(chunks):
                    landed(k, partner + 2 * before)
                process(z + before)

            return 0

        lax.fori_loop(1, Z + 1, step, 0)

        def drain(s, _):
            for k in range(chunks):

                @pl.when(z - s >= 0)
                def _():
                    block = me - 2 * s

                    @pl.when(z < Z - 1)
                    def _():
                        copy(k, block, 1).wait_send()

                    copy(k, block, 0).wait_send()

                    @pl.when((s == 0) & (z > 0))
                    def _():
                        copy(k, block, 2).wait_send()

                @pl.when((s > 0) & (z + s < Z))
                def _():
                    block = me + 2 * s

                    @pl.when(z > 0)
                    def _():
                        copy(k, block, 2).wait_send()

                    copy(k, block, 0).wait_send()

            return 0

        return lambda: lax.fori_loop(0, Z, drain, 0)

    heads = q_ref.shape[2]
    span = k_ref.shape[2]
    hd = q_ref.shape[3]

    def attend(g):
        scores = lax.dot_general(
            q_ref[:, g], k_ref[:, g], (((2,), (2,)), ((0,), (0,))), preferred_element_type=F32
        ) * (1.0 / math.sqrt(hd))
        slots = lax.broadcasted_iota(jnp.int32, (R, heads, span), 2)
        scores = jnp.where(slots < len_ref[...], scores, -1e30)
        top = jnp.max(scores, axis=-1, keepdims=True)
        weights = jnp.exp(scores - top)
        weights = (weights / jnp.sum(weights, axis=-1, keepdims=True)).astype(BF16)
        result = lax.dot_general(
            weights, v_ref[:, g], (((2,), (1,)), ((0,), (0,))), preferred_element_type=F32
        )
        mixed[...] = result.reshape(R * heads, hd)
        for j in range(heads):
            att[g, me, :, j * hd : (j + 1) * hd] = mixed[pl.ds(j, R, stride=heads), :].astype(BF16)

    drain_att = gather(
        lambda k, block: att.at[k, block], a_send, a_recv, G, attend, lambda chip: None
    )

    loads[0].wait()
    width = heads * hd

    def rows_of(ref_value):
        return ref_value.astype(F32).reshape(ROWS, ref_value.shape[-1]).astype(BF16)

    def hx_copy(k, i):
        return pltpu.make_async_remote_copy(
            src_ref=hx_out.at[k], dst_ref=hx_in.at[k, h],
            send_sem=hx_send.at[k, i], recv_sem=hx_recv.at[k, h],
            device_id={"hg": (h + i) % H}, device_id_type=MESH,
        )

    for k in range(NC):
        total = jnp.zeros((ROWS, NW), F32)
        for g in range(G):
            total = total + jnp.dot(
                rows_of(att[g]), wo[g * width : (g + 1) * width, k * NW : (k + 1) * NW],
                preferred_element_type=F32,
            )
        total = total.reshape(E, R, NW)
        hx_out[k] = total.astype(BF16)
        for i in range(1, H):
            hx_copy(k, i).start()
        proj[k] = total

    def res_landed(i, _):
        src = (me + i) % E
        pltpu.make_async_remote_copy(
            src_ref=resb.at[src], dst_ref=resb.at[src],
            send_sem=rs_send.at[src], recv_sem=rs_recv.at[src],
            device_id={"ep": src}, device_id_type=MESH,
        ).wait_recv()
        pltpu.make_async_remote_copy(
            src_ref=wbuf.at[src], dst_ref=wbuf.at[src],
            send_sem=sh_send.at[src], recv_sem=sh_recv.at[src],
            device_id={"ep": src}, device_id_type=MESH,
        ).wait_recv()
        return 0

    lax.fori_loop(1, E, res_landed, 0)

    def hidden_ready(k):
        value = proj[k] + resb[:, :, k * NW : (k + 1) * NW].astype(F32)
        for i in range(1, H):
            src = (h + i) % H
            pltpu.make_async_remote_copy(
                src_ref=hx_out.at[k], dst_ref=hx_in.at[k, src],
                send_sem=hx_send.at[k, i], recv_sem=hx_recv.at[k, src],
                device_id={"hg": src}, device_id_type=MESH,
            ).wait_recv()
            value = value + hx_in[k, src].astype(F32)
        hid[me * NC + k] = value.astype(BF16)

    acc_g[...] = jnp.zeros_like(acc_g)
    acc_u[...] = jnp.zeros_like(acc_u)
    ssq[...] = jnp.zeros_like(ssq)
    loads[1].wait()
    loads[2].wait()

    def experts_in(chip):
        def piece(i, _):
            p = chip * (2 * NC) + i
            start = pl.multiple_of(p * NW, NW)
            x = hid[p].astype(F32).reshape(ROWS, NW)
            ssq[...] += jnp.sum(x * x, axis=-1, keepdims=True)
            xb = (x * gain_ref[:, pl.ds(start, NW)]).astype(BF16)
            for j in range(J):
                acc_g[j] += jnp.dot(xb, wg[j, pl.ds(start, NW), :], preferred_element_type=F32)
                acc_u[j] += jnp.dot(xb, wu[j, pl.ds(start, NW), :], preferred_element_type=F32)
            return 0

        lax.fori_loop(0, 2 * NC, piece, 0)

    drain_hid = gather(
        lambda k, block: hid.at[block * NC + k], h_send, h_recv, NC, hidden_ready, experts_in
    )

    scale = lax.rsqrt(ssq[...] * (1.0 / D) + 1e-6)
    shares = wbuf[...].reshape(ROWS, wbuf.shape[2])
    lanes = lax.broadcasted_iota(jnp.int32, shares.shape, 1)
    for j in range(J):
        own = jnp.sum(jnp.where(lanes == me * J + j, shares, 0.0), axis=-1, keepdims=True)
        gate_value = acc_g[j] * scale
        up_value = acc_u[j] * (scale * own)
        act[j] = (gate_value * jax.nn.sigmoid(gate_value) * up_value).astype(BF16)

    loads[3].wait()

    def d1_copy(i, q):
        return pltpu.make_async_remote_copy(
            src_ref=d1_out.at[i, q], dst_ref=d1_in.at[i, q],
            send_sem=d1_send.at[i, q], recv_sem=d1_recv.at[i, q],
            device_id={"ep": partner}, device_id_type=MESH,
        )

    def d2_copy(i, q):
        return pltpu.make_async_remote_copy(
            src_ref=d2_out.at[i - 1, q], dst_ref=d2_in.at[i - 1, q],
            send_sem=d2_send.at[i - 1, q], recv_sem=d2_recv.at[i - 1, q],
            device_id={"hg": (h + i) % H}, device_id_type=MESH,
        )

    def d3_copy(i, q):
        there = (z + i) % Z
        return pltpu.make_async_remote_copy(
            src_ref=d3_out.at[q, there], dst_ref=d3_in.at[i - 1, q],
            send_sem=d3_send.at[i - 1, q], recv_sem=d3_recv.at[i - 1, q],
            device_id={"ep": there * 2 + c}, device_id_type=MESH,
        )

    def down(i, q):
        start = pl.multiple_of(((h + i) % H) * DH + q * QW, QW)
        total = jnp.zeros((ROWS, QW), F32)
        for j in range(J):
            total = total + jnp.dot(
                act[j], wd[j, :, pl.ds(start, QW)], preferred_element_type=F32
            )
        total = total.reshape(Z, 2, R, QW)
        first, second = total[:, 0], total[:, 1]
        d1_out[i, q] = jnp.where(c == 0, second, first).astype(BF16)
        d1_copy(i, q).start()
        mine[i, q] = jnp.where(c == 0, first, second)

    for q in range(Q):
        for i in range(1, H):
            down(i, q)
    for q in range(Q):
        down(0, q)
        for i in range(1, H):
            d1_copy(i, q).wait_recv()
            d2_out[i - 1, q] = (mine[i, q] + d1_in[i, q].astype(F32)).astype(BF16)
            d2_copy(i, q).start()

    for q in range(Q):
        d1_copy(0, q).wait_recv()
        total = mine[0, q] + d1_in[0, q].astype(F32)
        for i in range(1, H):
            d2_copy(i, q).wait_recv()
            total = total + d2_in[i - 1, q].astype(F32)
        mine[0, q] = total
        d3_out[q] = total.astype(BF16)
        for i in range(1, Z):
            d3_copy(i, q).start()

    per = QW // NW
    for q in range(Q):
        total = mine[0, q, z]
        for i in range(1, Z):
            d3_copy(i, q).wait_recv()
            total = total + d3_in[i - 1, q].astype(F32)
        for i in range(per):
            p = (h * DH + q * QW) // NW + i
            part = hid[p, me].astype(F32) + total[:, i * NW : (i + 1) * NW]
            out_ref[:, q * QW + i * NW : q * QW + (i + 1) * NW] = part.astype(BF16)

    drain_att()
    drain_hid()

    def spread_done(i, _):
        dst = (me + i) % E
        res_copy(dst).wait_send()
        share_copy(dst).wait_send()
        return 0

    lax.fori_loop(1, E, spread_done, 0)
    for k in range(NC):
        for i in range(1, H):
            hx_copy(k, i).wait_send()
    for q in range(Q):
        for i in range(H):
            d1_copy(i, q).wait_send()
        for i in range(1, H):
            d2_copy(i, q).wait_send()
        for i in range(1, Z):
            d3_copy(i, q).wait_send()


def shards(
    queries,
    key_cache,
    value_cache,
    lengths,
    residual,
    out_weight,
    norm_gain,
    routes,
    route_probs,
    gate_weight,
    up_weight,
    down_weight,
):
    E = lax.axis_size("ep")
    H = lax.axis_size("hg")
    batches, rows, heads, hd = queries.shape
    G, span = key_cache.shape[2], key_cache.shape[3]
    R = batches * rows
    D = residual.shape[2]
    J, _, hid_local = gate_weight.shape
    CB = D // E
    NC = 2 if CB % 256 == 0 else 1
    NW = CB // NC
    DH = D // H
    Q = max(1, DH // 512)
    QW = DH // Q
    Z = E // 2
    ROWS = E * R
    lane_count = -(-J * E // 128) * 128
    width = heads // G * hd
    dims = (E, H, G, R, NC, NW, Q, QW, J)
    vmem = pl.BlockSpec(memory_space=pltpu.VMEM)
    hbm = pl.BlockSpec(memory_space=pl.ANY)
    dma = pltpu.SemaphoreType.DMA
    out = pl.pallas_call(
        functools.partial(layer_kernel, dims),
        out_shape=jax.ShapeDtypeStruct((R, DH), BF16),
        in_specs=[vmem] * 8 + [hbm] * 4,
        out_specs=vmem,
        scratch_shapes=[
            pltpu.VMEM(out_weight.shape, BF16),
            pltpu.VMEM(gate_weight.shape, BF16),
            pltpu.VMEM(up_weight.shape, BF16),
            pltpu.VMEM(down_weight.shape, BF16),
            pltpu.VMEM((R * (heads // G), hd), F32),
            pltpu.VMEM((G, E, R, width), BF16),
            pltpu.VMEM((E, R, CB), BF16),
            pltpu.VMEM((E, R, lane_count), F32),
            pltpu.VMEM((NC, E, R, NW), F32),
            pltpu.VMEM((NC, E, R, NW), BF16),
            pltpu.VMEM((NC, H, E, R, NW), BF16),
            pltpu.VMEM((E * NC, E, R, NW), BF16),
            pltpu.VMEM((J, ROWS, hid_local), F32),
            pltpu.VMEM((J, ROWS, hid_local), F32),
            pltpu.VMEM((ROWS, 1), F32),
            pltpu.VMEM((J, ROWS, hid_local), BF16),
            pltpu.VMEM((H, Q, Z, R, QW), F32),
            pltpu.VMEM((H, Q, Z, R, QW), BF16),
            pltpu.VMEM((H, Q, Z, R, QW), BF16),
            pltpu.VMEM((H - 1, Q, Z, R, QW), BF16),
            pltpu.VMEM((H - 1, Q, Z, R, QW), BF16),
            pltpu.VMEM((Q, Z, R, QW), BF16),
            pltpu.VMEM((Z - 1, Q, R, QW), BF16),
            dma((4,)),
            dma((E,)), dma((E,)), dma((E,)), dma((E,)),
            dma((G, E, 3)), dma((G, E)),
            dma((NC, H)), dma((NC, H)),
            dma((NC, E, 3)), dma((NC, E)),
            dma((H, Q)), dma((H, Q)),
            dma((H - 1, Q)), dma((H - 1, Q)),
            dma((Z - 1, Q)), dma((Z - 1, Q)),
        ],
        compiler_params=pltpu.CompilerParams(
            collective_id=0, has_side_effects=True, vmem_limit_bytes=60 * 1024 * 1024
        ),
        name="layer",
    )(
        queries.reshape(R, G, heads // G, hd),
        key_cache.reshape(R, G, span, hd),
        value_cache.reshape(R, G, span, hd),
        lengths.reshape(R, 1, 1),
        residual.reshape(R, D),
        norm_gain.reshape(1, D),
        routes.reshape(R, routes.shape[2]),
        route_probs.reshape(R, route_probs.shape[2]),
        out_weight,
        gate_weight,
        up_weight,
        down_weight,
    )
    return out.reshape(batches, rows, DH)


def solution(mesh):
    return jax.shard_map(
        shards,
        mesh=mesh,
        in_specs=(
            P(None, ("groups", "ep"), "hg", None),
            P(None, ("groups", "ep"), "hg", None, None),
            P(None, ("groups", "ep"), "hg", None, None),
            P(None, ("groups", "ep")),
            P(None, ("groups", "ep"), None),
            P("hg", "ep"),
            P(),
            P(None, ("groups", "ep"), None),
            P(None, ("groups", "ep"), None),
            P("ep", None, "hg"),
            P("ep", None, "hg"),
            P("ep", "hg", None),
        ),
        out_specs=P(None, ("groups", "ep"), "hg"),
        check_vma=False,
    )
```

time: 319 us -> 72.4 us (0.23)
  blocking collectives: 136 us -> 0 us
  waiting for transfers between devices: 75.6 us -> 0 us
  Pallas kernels: 0 us -> 69.3 us
  matrix products: 51.8 us -> 0 us
  starting transfers between devices: 23.5 us -> 0 us
  between operations: 13.5 us -> 0.01 us
  other arithmetic: 8.09 us -> 0 us
  local copies, waits for them, and re-layouts: 9.37 us -> 2.91 us
    all_to_all x3 -> x0, blocking collectives: 89 us -> none  [shards(): lax.all_to_all(buffer, 'ep', split_axis=1, concat_axis=1, tiled=True)]
    pallas_call x0 -> x1, Pallas kernels: none -> 69.3 us  [shards(): pl.pallas_call(functools.partial(layer_kernel, dims), out_shape=jax.Shape...]
    dot_general x21 -> x0, matrix products: 51.8 us -> none  [the longest x3 24.2 us: shards(): jnp.einsum('bsjch,jhd->bsjcd', activation, down_weight, preferred_element...]
    all_gather x3 -> x0, blocking collectives: 46.7 us -> none  [shards(): lax.all_gather(attended, 'ep', axis=1, tiled=True)]
    all_to_all x6 -> x0, waiting for transfers between devices: 45.6 us -> none  [the longest x3 35.3 us: shards(): lax.all_to_all(summed, 'ep', split_axis=1, concat_axis=1, tiled=True)]
    psum x1 -> x0, waiting for transfers between devices: 24.7 us -> none  [shards(): projected = lax.psum(own_rows, 'hg')]
    all_to_all x6 -> x0, starting transfers between devices: 23.3 us -> none  [the longest x3 12.8 us: shards(): lax.all_to_all(partial_value, 'ep', split_axis=1, concat_axis=2, tiled=True)]
    reduce_scatter x3 -> x0, waiting for transfers between devices: 5.27 us -> none  [shards(): lax.psum_scatter(partial_out, 'hg', scatter_dimension=4, tiled=True)]
  transfers between devices with their start and end apart: 10 -> 0, of which waited for: 7 -> 0; matrix products, arithmetic and copies ran while one was open for 14% -> 0% of each run, Pallas kernels for 0% -> 0%
where the time goes in v1:
time: 72.4 us; the launch traced here: 72.2 us
  Pallas kernels  69.3 us (96%)
  local copies, waits for them, and re-layouts  2.91 us (4%)
    pallas_call x1, Pallas kernels, shards(): pl.pallas_call(functools.partial(layer_kernel, dims), out_shape=jax.Shape...  69.3 us
    unnamed x1, local copies, waits for them, and re-layouts  1.54 us

profile of v1, /device:TPU:0, one launch (start us, length us, event | category | flops | bytes accessed | tf_op | source)
XLA Modules:
  0.0 72.2 jit_solution(12503215313287745114)
XLA Ops:
  0.0 1.4 %reshape.36.len_ref = s32[24,1,1]{2,1,0:T(1,128)} reshape(s32[3,8]{1,0:T(4,128)} %param.15) | data formatting | bytes 192 | tf_op jit(solution)/shard_map/reshape | solution.py:478
  1.4 69.3 %layer.1 = bf16[24,2048]{1,0:T(8,128)(2,1)} custom-call(bf16[24,2,16,128]{3,2,1,0:T(8,128)(2,1)} %bitcast.11, bf16[24,2,96,128]{3,2,1,0:T(8,128)(2,1)} %bitcast.8, bf16[24,2,96,128]{3,2,1,0:T(8,128)(2,1)} %bitcast.9, s32[24,1,1]{2,1,0:T(1,128)} %reshape.36.len_ref, bf16[24,4096]{1,0:T(8,128)(2,1)} %bitcast.12, f32[1,4096]{1,0:T(1,128)} %bitcast.13, ...), custom_call_target="tpu_custom_call" | custom-call | tf_op jit(solution)/shard_map/layer/pallas_call | solution.py:432
  70.6 1.5 %copy.15 = bf16[3,8,2048]{2,1,0:T(8,128)(2,1)} copy(bf16[3,8,2048]{2,1,0:T(8,128)(2,1)} %bitcast.10) | data formatting | bytes 196608

commit v2 on v1

--- a/solution.py
+++ b/solution.py
@@ -15,15 +15,15 @@
 
 def layer_kernel(
     dims,
-    q_ref, k_ref, v_ref, len_ref, res_ref, gain_ref, routes_ref, probs_ref,
-    wo_hbm, wg_hbm, wu_hbm, wd_hbm,
+    len_ref, res_ref, gain_ref, routes_ref, probs_ref,
+    q_hbm, k_hbm, v_hbm, wo_hbm, wg_hbm, wu_hbm, wd_hbm,
     out_ref,
-    wo, wg, wu, wd, mixed, att, resb, wbuf, proj, hx_out, hx_in, hid,
+    q_ref, k_ref, v_ref, wo, wg, wu, wd, mixed, att, resb, wbuf, hx_out, hx_in, hid,
     acc_g, acc_u, ssq, act, mine, d1_out, d1_in, d2_out, d2_in, d3_out, d3_in,
     w_sem, rs_send, rs_recv, sh_send, sh_recv, a_send, a_recv, hx_send, hx_recv,
     h_send, h_recv, d1_send, d1_recv, d2_send, d2_recv, d3_send, d3_recv,
 ):
-    E, H, G, R, NC, NW, Q, QW, J = dims
+    E, H, G, R, Q, QW, J, packed = dims
     Z = E // 2
     ROWS = E * R
     D = res_ref.shape[1]
@@ -34,6 +34,10 @@
     z = me // 2
     c = me % 2
     partner = z * 2 + (1 - c)
+    PER = E // H
+
+    def pos(e):
+        return (e % H) * PER + e // H
 
     barrier = pltpu.get_barrier_semaphore()
 
@@ -50,7 +54,7 @@
 
     loads = [
         pltpu.make_async_copy(src, dst, w_sem.at[i])
-        for i, (src, dst) in enumerate(((wo_hbm, wo), (wg_hbm, wg), (wu_hbm, wu), (wd_hbm, wd)))
+        for i, (src, dst) in enumerate(((k_hbm, k_ref), (v_hbm, v_ref), (q_hbm, q_ref), (wo_hbm, wo), (wg_hbm, wg), (wu_hbm, wu), (wd_hbm, wd)))
     ]
     for load in loads:
         load.start()
@@ -58,36 +62,48 @@
     probs = probs_ref[...]
     share = probs / jnp.sum(probs, axis=-1, keepdims=True)
     routes = routes_ref[...]
-    lanes = lax.broadcasted_iota(jnp.int32, (R, wbuf.shape[2]), 1)
-    dense = jnp.zeros((R, wbuf.shape[2]), F32)
+    lanes = lax.broadcasted_iota(jnp.int32, (R, 128), 1)
+    named = lanes % (E * J) if packed else lanes
+    dense = jnp.zeros((R, 128), F32)
     for t in range(routes.shape[1]):
-        dense = dense + jnp.where(lanes == routes[:, t : t + 1], share[:, t : t + 1], 0.0)
-    wbuf[me] = dense
+        dense = dense + jnp.where(named == routes[:, t : t + 1], share[:, t : t + 1], 0.0)
+    if packed:
+        row_in_eight = lax.broadcasted_iota(jnp.int32, (R, 128), 0) % 8
+        dense = jnp.where(lanes // (E * J) == row_in_eight, dense, 0.0)
+        dense = jnp.sum(dense.reshape(R // 8, 8, 128), axis=1)
+    wbuf[pos(me)] = dense
 
     pl.semaphore_wait(barrier, E - 1 + H - 1)
 
     def share_copy(dst):
         return pltpu.make_async_remote_copy(
-            src_ref=wbuf.at[me], dst_ref=wbuf.at[me],
+            src_ref=wbuf.at[pos(me)], dst_ref=wbuf.at[pos(me)],
             send_sem=sh_send.at[dst], recv_sem=sh_recv.at[me],
             device_id={"ep": dst}, device_id_type=MESH,
         )
 
     def res_copy(dst):
         return pltpu.make_async_remote_copy(
-            src_ref=res_ref.at[:, pl.ds(pl.multiple_of(dst * CB, CB), CB)], dst_ref=resb.at[me],
+            src_ref=res_ref.at[:, pl.ds(pl.multiple_of(dst * CB, CB), CB)], dst_ref=resb.at[me // H],
             send_sem=rs_send.at[dst], recv_sem=rs_recv.at[me],
             device_id={"ep": dst}, device_id_type=MESH,
         )
 
     def spread(i, _):
         dst = (me + i) % E
-        res_copy(dst).start()
+
+        @pl.when(h == me % H)
+        def _():
+            res_copy(dst).start()
+
         share_copy(dst).start()
         return 0
 
     lax.fori_loop(1, E, spread, 0)
-    resb[me] = res_ref[:, pl.ds(pl.multiple_of(me * CB, CB), CB)]
+
+    @pl.when(h == me % H)
+    def _():
+        resb[me // H] = res_ref[:, pl.ds(pl.multiple_of(me * CB, CB), CB)]
 
     def gather(place, send, recv, chunks, own_ready, process):
         def copy(k, block, way):
@@ -196,12 +212,20 @@
     span = k_ref.shape[2]
     hd = q_ref.shape[3]
 
+    loads[0].wait()
+    loads[1].wait()
+    loads[2].wait()
+    rows = R // len_ref.shape[0]
+    live = jnp.stack(
+        [jnp.full((heads, span), len_ref[r // rows, r % rows], jnp.int32) for r in range(R)]
+    )
+
     def attend(g):
         scores = lax.dot_general(
             q_ref[:, g], k_ref[:, g], (((2,), (2,)), ((0,), (0,))), preferred_element_type=F32
         ) * (1.0 / math.sqrt(hd))
         slots = lax.broadcasted_iota(jnp.int32, (R, heads, span), 2)
-        scores = jnp.where(slots < len_ref[...], scores, -1e30)
+        scores = jnp.where(slots < live, scores, -1e30)
         top = jnp.max(scores, axis=-1, keepdims=True)
         weights = jnp.exp(scores - top)
         weights = (weights / jnp.sum(weights, axis=-1, keepdims=True)).astype(BF16)
@@ -210,100 +234,182 @@
         )
         mixed[...] = result.reshape(R * heads, hd)
         for j in range(heads):
-            att[g, me, :, j * hd : (j + 1) * hd] = mixed[pl.ds(j, R, stride=heads), :].astype(BF16)
+            att[g, pos(me), :, j * hd : (j + 1) * hd] = mixed[pl.ds(j, R, stride=heads), :].astype(BF16)
 
     drain_att = gather(
-        lambda k, block: att.at[k, block], a_send, a_recv, G, attend, lambda chip: None
+        lambda k, block: att.at[k, pos(block)], a_send, a_recv, G, attend, lambda chip: None
     )
 
-    loads[0].wait()
+    loads[3].wait()
     width = heads * hd
 
-    def rows_of(ref_value):
-        return ref_value.astype(F32).reshape(ROWS, ref_value.shape[-1]).astype(BF16)
-
-    def hx_copy(k, i):
-        return pltpu.make_async_remote_copy(
-            src_ref=hx_out.at[k], dst_ref=hx_in.at[k, h],
-            send_sem=hx_send.at[k, i], recv_sem=hx_recv.at[k, h],
-            device_id={"hg": (h + i) % H}, device_id_type=MESH,
-        )
-
-    for k in range(NC):
-        total = jnp.zeros((ROWS, NW), F32)
+    def project(part):
+        total = jnp.zeros((PER * R, CB), F32)
         for g in range(G):
+            rows_in = att[g, pl.ds(part * PER, PER)].astype(F32).reshape(PER * R, width)
             total = total + jnp.dot(
-                rows_of(att[g]), wo[g * width : (g + 1) * width, k * NW : (k + 1) * NW],
+                rows_in.astype(BF16), wo[g * width : (g + 1) * width, :],
                 preferred_element_type=F32,
             )
-        total = total.reshape(E, R, NW)
-        hx_out[k] = total.astype(BF16)
-        for i in range(1, H):
-            hx_copy(k, i).start()
-        proj[k] = total
-
-    def res_landed(i, _):
+        return total.reshape(PER, R, CB)
+
+    def hx_copy(i):
+        return pltpu.make_async_remote_copy(
+            src_ref=hx_out.at[i - 1], dst_ref=hx_in.at[i - 1],
+            send_sem=hx_send.at[i - 1], recv_sem=hx_recv.at[i - 1],
+            device_id={"hg": (h + i) % H}, device_id_type=MESH,
+        )
+
+    for i in range(1, H):
+        hx_out[i - 1] = project((h + i) % H).astype(BF16)
+        hx_copy(i).start()
+    own_part = project(h)
+
+    def landed_at(ref, place, sem):
+        pltpu.make_async_remote_copy(
+            src_ref=ref.at[place], dst_ref=ref.at[place],
+            send_sem=sem, recv_sem=sem,
+            device_id={"ep": partner}, device_id_type=MESH,
+        ).wait_recv()
+
+    def spread_landed(i, _):
         src = (me + i) % E
-        pltpu.make_async_remote_copy(
-            src_ref=resb.at[src], dst_ref=resb.at[src],
-            send_sem=rs_send.at[src], recv_sem=rs_recv.at[src],
-            device_id={"ep": src}, device_id_type=MESH,
-        ).wait_recv()
-        pltpu.make_async_remote_copy(
-            src_ref=wbuf.at[src], dst_ref=wbuf.at[src],
-            send_sem=sh_send.at[src], recv_sem=sh_recv.at[src],
-            device_id={"ep": src}, device_id_type=MESH,
-        ).wait_recv()
+
+        @pl.when(src % H == h)
+        def _():
+            landed_at(resb, src // H, rs_recv.at[src])
+
+        landed_at(wbuf, pos(src), sh_recv.at[src])
         return 0
 
-    lax.fori_loop(1, E, res_landed, 0)
-
-    def hidden_ready(k):
-        value = proj[k] + resb[:, :, k * NW : (k + 1) * NW].astype(F32)
-        for i in range(1, H):
-            src = (h + i) % H
-            pltpu.make_async_remote_copy(
-                src_ref=hx_out.at[k], dst_ref=hx_in.at[k, src],
-                send_sem=hx_send.at[k, i], recv_sem=hx_recv.at[k, src],
-                device_id={"hg": src}, device_id_type=MESH,
-            ).wait_recv()
-            value = value + hx_in[k, src].astype(F32)
-        hid[me * NC + k] = value.astype(BF16)
+    lax.fori_loop(1, E, spread_landed, 0)
+    own_part = own_part + resb[...].astype(F32)
+    for i in range(1, H):
+        hx_copy(i).wait_recv()
+        own_part = own_part + hx_in[i - 1].astype(F32)
+    hid[me, h] = own_part.astype(BF16)
 
     acc_g[...] = jnp.zeros_like(acc_g)
     acc_u[...] = jnp.zeros_like(acc_u)
     ssq[...] = jnp.zeros_like(ssq)
-    loads[1].wait()
-    loads[2].wait()
+    loads[4].wait()
+    loads[5].wait()
 
     def experts_in(chip):
         def piece(i, _):
-            p = chip * (2 * NC) + i
-            start = pl.multiple_of(p * NW, NW)
-            x = hid[p].astype(F32).reshape(ROWS, NW)
+            p = chip * 2 + i
+            start = pl.multiple_of(p * CB, CB)
+            x = hid[p].astype(F32).reshape(ROWS, CB)
             ssq[...] += jnp.sum(x * x, axis=-1, keepdims=True)
-            xb = (x * gain_ref[:, pl.ds(start, NW)]).astype(BF16)
+            xb = (x * gain_ref[:, pl.ds(start, CB)]).astype(BF16)
             for j in range(J):
-                acc_g[j] += jnp.dot(xb, wg[j, pl.ds(start, NW), :], preferred_element_type=F32)
-                acc_u[j] += jnp.dot(xb, wu[j, pl.ds(start, NW), :], preferred_element_type=F32)
+                acc_g[j] += jnp.dot(xb, wg[j, pl.ds(start, CB), :], preferred_element_type=F32)
+                acc_u[j] += jnp.dot(xb, wu[j, pl.ds(start, CB), :], preferred_element_type=F32)
             return 0
 
-        lax.fori_loop(0, 2 * NC, piece, 0)
-
-    drain_hid = gather(
-        lambda k, block: hid.at[block * NC + k], h_send, h_recv, NC, hidden_ready, experts_in
-    )
+        lax.fori_loop(0, 2, piece, 0)
+
+    def hid_copy(block, part, way):
+        if way < 3:
+            device = {"ep": (partner, me + 2, me - 2)[way]}
+        else:
+            device = {"hg": (h + way - 2) % H}
+        return pltpu.make_async_remote_copy(
+            src_ref=hid.at[block, part], dst_ref=hid.at[block, part],
+            send_sem=h_send.at[block, part, way], recv_sem=h_recv.at[block, part],
+            device_id=device, device_id_type=MESH,
+        )
+
+    def hid_pass(block, go, right, left):
+        for way, wanted in ((1, right), (2, left)):
+            if wanted is not False:
+
+                @pl.when(wanted)
+                def _():
+                    go(hid_copy(block, h, way))
+
+        for i in range(1, H):
+            go(hid_copy(block, h, 2 + i))
+        go(hid_copy(block, h, 0))
+
+    def hid_cross(block, go, wait):
+        for i in range(1, H):
+            part = (h + i) % H
+            if wait:
+                hid_copy(block, part, 0).wait_recv()
+            go(hid_copy(block, part, 0))
+
+    def hid_take(chip):
+        for part in range(H):
+            hid_copy(chip * 2 + (1 - c), part, 0).wait_recv()
+        experts_in(chip)
+
+    def sides(s, action):
+        @pl.when((s >= 0) & (z - s >= 0))
+        def _():
+            action(z - s, True)
+
+        @pl.when((s > 0) & (z + s < Z))
+        def _():
+            action(z + s, False)
+
+    def start(copy):
+        copy.start()
+
+    def sent(copy):
+        copy.wait_send()
+
+    hid_pass(me, start, z < Z - 1, z > 0)
+
+    def hid_step(s, _):
+        def forward(chip, from_left):
+            block = chip * 2 + c
+            hid_copy(block, h, 0).wait_recv()
+            hid_pass(block, start, (z < Z - 1) if from_left else False, False if from_left else (z > 0))
+
+        sides(s, forward)
+        sides(s - 1, lambda chip, from_left: hid_cross(chip * 2 + c, start, True))
+        sides(s - 2, lambda chip, from_left: hid_take(chip))
+        return 0
+
+    lax.fori_loop(1, Z + 2, hid_step, 0)
+
+    def drain_hid():
+        hid_pass(me, sent, z < Z - 1, z > 0)
+
+        def drain(s, _):
+            def passed(chip, from_left):
+                hid_pass(
+                    chip * 2 + c, sent, (z < Z - 1) if from_left else False, False if from_left else (z > 0)
+                )
+
+            @pl.when(s > 0)
+            def _():
+                sides(s, passed)
+
+            sides(s, lambda chip, from_left: hid_cross(chip * 2 + c, sent, False))
+            return 0
+
+        lax.fori_loop(0, Z, drain, 0)
 
     scale = lax.rsqrt(ssq[...] * (1.0 / D) + 1e-6)
-    shares = wbuf[...].reshape(ROWS, wbuf.shape[2])
-    lanes = lax.broadcasted_iota(jnp.int32, shares.shape, 1)
+    shares = wbuf[...]
+    if packed:
+        shares = jnp.broadcast_to(
+            shares.reshape(E * R // 8, 1, 128), (E * R // 8, 8, 128)
+        )
+    shares = shares.reshape(ROWS, 128)
+    lanes = lax.broadcasted_iota(jnp.int32, (ROWS, 128), 1)
+    offset = (lax.broadcasted_iota(jnp.int32, (ROWS, 128), 0) % 8) * (E * J) if packed else 0
     for j in range(J):
-        own = jnp.sum(jnp.where(lanes == me * J + j, shares, 0.0), axis=-1, keepdims=True)
+        own = jnp.sum(
+            jnp.where(lanes == offset + (me * J + j), shares, 0.0), axis=-1, keepdims=True
+        )
         gate_value = acc_g[j] * scale
         up_value = acc_u[j] * (scale * own)
         act[j] = (gate_value * jax.nn.sigmoid(gate_value) * up_value).astype(BF16)
 
-    loads[3].wait()
+    loads[6].wait()
 
     def d1_copy(i, q):
         return pltpu.make_async_remote_copy(
@@ -319,10 +425,13 @@
             device_id={"hg": (h + i) % H}, device_id_type=MESH,
         )
 
+    def chip_place(chip):
+        return (chip % (H // 2)) * PER + chip // (H // 2)
+
     def d3_copy(i, q):
         there = (z + i) % Z
         return pltpu.make_async_remote_copy(
-            src_ref=d3_out.at[q, there], dst_ref=d3_in.at[i - 1, q],
+            src_ref=d3_out.at[q, chip_place(there)], dst_ref=d3_in.at[i - 1, q],
             send_sem=d3_send.at[i - 1, q], recv_sem=d3_recv.at[i - 1, q],
             device_id={"ep": there * 2 + c}, device_id_type=MESH,
         )
@@ -334,8 +443,9 @@
             total = total + jnp.dot(
                 act[j], wd[j, :, pl.ds(start, QW)], preferred_element_type=F32
             )
-        total = total.reshape(Z, 2, R, QW)
-        first, second = total[:, 0], total[:, 1]
+        total = total.reshape(H // 2, 2, PER, R, QW)
+        first = total[:, 0].reshape(Z, R, QW)
+        second = total[:, 1].reshape(Z, R, QW)
         d1_out[i, q] = jnp.where(c == 0, second, first).astype(BF16)
         d1_copy(i, q).start()
         mine[i, q] = jnp.where(c == 0, first, second)
@@ -361,30 +471,34 @@
         for i in range(1, Z):
             d3_copy(i, q).start()
 
-    per = QW // NW
+    part_width = min(CB, QW)
     for q in range(Q):
-        total = mine[0, q, z]
+        total = mine[0, q, chip_place(z)]
         for i in range(1, Z):
             d3_copy(i, q).wait_recv()
             total = total + d3_in[i - 1, q].astype(F32)
-        for i in range(per):
-            p = (h * DH + q * QW) // NW + i
-            part = hid[p, me].astype(F32) + total[:, i * NW : (i + 1) * NW]
-            out_ref[:, q * QW + i * NW : q * QW + (i + 1) * NW] = part.astype(BF16)
+        for i in range(QW // part_width):
+            column = i * part_width
+            p = (h * DH + q * QW + column) // CB
+            part = hid[p, me % H, me // H].astype(F32) + total[:, column : column + part_width]
+            out_ref[:, q * QW + column : q * QW + column + part_width] = part.astype(BF16)
 
     drain_att()
     drain_hid()
 
     def spread_done(i, _):
         dst = (me + i) % E
-        res_copy(dst).wait_send()
+
+        @pl.when(h == me % H)
+        def _():
+            res_copy(dst).wait_send()
+
         share_copy(dst).wait_send()
         return 0
 
     lax.fori_loop(1, E, spread_done, 0)
-    for k in range(NC):
-        for i in range(1, H):
-            hx_copy(k, i).wait_send()
+    for i in range(1, H):
+        hx_copy(i).wait_send()
     for q in range(Q):
         for i in range(H):
             d1_copy(i, q).wait_send()
@@ -416,37 +530,39 @@
     D = residual.shape[2]
     J, _, hid_local = gate_weight.shape
     CB = D // E
-    NC = 2 if CB % 256 == 0 else 1
-    NW = CB // NC
     DH = D // H
     Q = max(1, DH // 512)
     QW = DH // Q
+    PER = E // H
+    packed = J * E * 8 == 128 and R % 8 == 0
     Z = E // 2
     ROWS = E * R
-    lane_count = -(-J * E // 128) * 128
+    share_rows = R // 8 if packed else R
     width = heads // G * hd
-    dims = (E, H, G, R, NC, NW, Q, QW, J)
+    dims = (E, H, G, R, Q, QW, J, packed)
     vmem = pl.BlockSpec(memory_space=pltpu.VMEM)
     hbm = pl.BlockSpec(memory_space=pl.ANY)
     dma = pltpu.SemaphoreType.DMA
     out = pl.pallas_call(
         functools.partial(layer_kernel, dims),
         out_shape=jax.ShapeDtypeStruct((R, DH), BF16),
-        in_specs=[vmem] * 8 + [hbm] * 4,
+        in_specs=[pl.BlockSpec(memory_space=pltpu.SMEM)] + [vmem] * 4 + [hbm] * 7,
         out_specs=vmem,
         scratch_shapes=[
+            pltpu.VMEM((R, G, heads // G, hd), BF16),
+            pltpu.VMEM((R, G, span, hd), BF16),
+            pltpu.VMEM((R, G, span, hd), BF16),
             pltpu.VMEM(out_weight.shape, BF16),
             pltpu.VMEM(gate_weight.shape, BF16),
             pltpu.VMEM(up_weight.shape, BF16),
             pltpu.VMEM(down_weight.shape, BF16),
             pltpu.VMEM((R * (heads // G), hd), F32),
             pltpu.VMEM((G, E, R, width), BF16),
-            pltpu.VMEM((E, R, CB), BF16),
-            pltpu.VMEM((E, R, lane_count), F32),
-            pltpu.VMEM((NC, E, R, NW), F32),
-            pltpu.VMEM((NC, E, R, NW), BF16),
-            pltpu.VMEM((NC, H, E, R, NW), BF16),
-            pltpu.VMEM((E * NC, E, R, NW), BF16),
+            pltpu.VMEM((PER, R, CB), BF16),
+            pltpu.VMEM((E, share_rows, 128), F32),
+            pltpu.VMEM((H - 1, PER, R, CB), BF16),
+            pltpu.VMEM((H - 1, PER, R, CB), BF16),
+            pltpu.VMEM((E, H, PER, R, CB), BF16),
             pltpu.VMEM((J, ROWS, hid_local), F32),
             pltpu.VMEM((J, ROWS, hid_local), F32),
             pltpu.VMEM((ROWS, 1), F32),
@@ -458,11 +574,11 @@
             pltpu.VMEM((H - 1, Q, Z, R, QW), BF16),
             pltpu.VMEM((Q, Z, R, QW), BF16),
             pltpu.VMEM((Z - 1, Q, R, QW), BF16),
-            dma((4,)),
+            dma((7,)),
             dma((E,)), dma((E,)), dma((E,)), dma((E,)),
             dma((G, E, 3)), dma((G, E)),
-            dma((NC, H)), dma((NC, H)),
-            dma((NC, E, 3)), dma((NC, E)),
+            dma((H - 1,)), dma((H - 1,)),
+            dma((E, H, H + 2)), dma((E, H)),
             dma((H, Q)), dma((H, Q)),
             dma((H - 1, Q)), dma((H - 1, Q)),
             dma((Z - 1, Q)), dma((Z - 1, Q)),
@@ -472,14 +588,14 @@
         ),
         name="layer",
     )(
-        queries.reshape(R, G, heads // G, hd),
-        key_cache.reshape(R, G, span, hd),
-        value_cache.reshape(R, G, span, hd),
-        lengths.reshape(R, 1, 1),
+        lengths,
         residual.reshape(R, D),
         norm_gain.reshape(1, D),
         routes.reshape(R, routes.shape[2]),
         route_probs.reshape(R, route_probs.shape[2]),
+        queries.reshape(R, G, heads // G, hd),
+        key_cache.reshape(R, G, span, hd),
+        value_cache.reshape(R, G, span, hd),
         out_weight,
         gate_weight,
         up_weight,

time: 72.4 us -> 67.3 us (0.930)
  Pallas kernels: 69.3 us -> 65.6 us
  local copies, waits for them, and re-layouts: 2.91 us -> 1.54 us
    pallas_call x1, Pallas kernels: 69.3 us -> 65.6 us  [shards(): pl.pallas_call(functools.partial(layer_kernel, dims), out_shape=jax.Shape...]
    reshape x1 -> x0, local copies, waits for them, and re-layouts: 1.37 us -> none  [shards(): lengths.reshape(R, 1, 1)]
where the time goes in v2:
time: 67.3 us; the launch traced here: 67.1 us
  Pallas kernels  65.6 us (97%)
  local copies, waits for them, and re-layouts  1.54 us (2%)
    pallas_call x1, Pallas kernels, shards(): pl.pallas_call(functools.partial(layer_kernel, dims), out_shape=jax.Shape...  65.6 us
    unnamed x1, local copies, waits for them, and re-layouts  1.54 us

profile of v2, /device:TPU:0, one launch (start us, length us, event | category | flops | bytes accessed | tf_op | source)
XLA Modules:
  0.0 67.1 jit_solution(1965635809621754480)
XLA Ops:
  0.0 65.6 %layer.1 = bf16[24,2048]{1,0:T(8,128)(2,1)} custom-call(s32[3,8]{1,0:T(4,128)} %len_ref.1, bf16[24,4096]{1,0:T(8,128)(2,1)} %bitcast.11, f32[1,4096]{1,0:T(1,128)} %bitcast.13, s32[24,8]{1,0:T(8,128)} %bitcast.14, f32[24,8]{1,0:T(8,128)} %bitcast.15, bf16[24,2,16,128]{3,2,1,0:T(8,128)(2,1)} %bitcast.12, bf16[24,2,96,128]{3,2,1,0:T(8,128)(2,1)} %bitcast.8, ...), custom_call_target="tpu_custom_call" | custom-call | tf_op jit(solution)/shard_map/layer/pallas_call | solution.py:546
  65.6 1.5 %copy.14 = bf16[3,8,2048]{2,1,0:T(8,128)(2,1)} copy(bf16[3,8,2048]{2,1,0:T(8,128)(2,1)} %bitcast.10) | data formatting | bytes 196608

commit v3 on v2

--- a/solution.py
+++ b/solution.py
@@ -23,7 +23,7 @@
     w_sem, rs_send, rs_recv, sh_send, sh_recv, a_send, a_recv, hx_send, hx_recv,
     h_send, h_recv, d1_send, d1_recv, d2_send, d2_recv, d3_send, d3_recv,
 ):
-    E, H, G, R, Q, QW, J, packed = dims
+    E, H, G, R, Q, QW, J, packed, SA, S = dims
     Z = E // 2
     ROWS = E * R
     D = res_ref.shape[1]
@@ -73,141 +73,6 @@
         dense = jnp.sum(dense.reshape(R // 8, 8, 128), axis=1)
     wbuf[pos(me)] = dense
 
-    pl.semaphore_wait(barrier, E - 1 + H - 1)
-
-    def share_copy(dst):
-        return pltpu.make_async_remote_copy(
-            src_ref=wbuf.at[pos(me)], dst_ref=wbuf.at[pos(me)],
-            send_sem=sh_send.at[dst], recv_sem=sh_recv.at[me],
-            device_id={"ep": dst}, device_id_type=MESH,
-        )
-
-    def res_copy(dst):
-        return pltpu.make_async_remote_copy(
-            src_ref=res_ref.at[:, pl.ds(pl.multiple_of(dst * CB, CB), CB)], dst_ref=resb.at[me // H],
-            send_sem=rs_send.at[dst], recv_sem=rs_recv.at[me],
-            device_id={"ep": dst}, device_id_type=MESH,
-        )
-
-    def spread(i, _):
-        dst = (me + i) % E
-
-        @pl.when(h == me % H)
-        def _():
-            res_copy(dst).start()
-
-        share_copy(dst).start()
-        return 0
-
-    lax.fori_loop(1, E, spread, 0)
-
-    @pl.when(h == me % H)
-    def _():
-        resb[me // H] = res_ref[:, pl.ds(pl.multiple_of(me * CB, CB), CB)]
-
-    def gather(place, send, recv, chunks, own_ready, process):
-        def copy(k, block, way):
-            target = (partner, me + 2, me - 2)[way]
-            return pltpu.make_async_remote_copy(
-                src_ref=place(k, block), dst_ref=place(k, block),
-                send_sem=send.at[k, block, way], recv_sem=recv.at[k, block],
-                device_id={"ep": target}, device_id_type=MESH,
-            )
-
-        def landed(k, block):
-            pltpu.make_async_remote_copy(
-                src_ref=place(k, block), dst_ref=place(k, block),
-                send_sem=send.at[k, block, 0], recv_sem=recv.at[k, block],
-                device_id={"ep": partner}, device_id_type=MESH,
-            ).wait_recv()
-
-        for k in range(chunks):
-            own_ready(k)
-
-            @pl.when(z < Z - 1)
-            def _():
-                copy(k, me, 1).start()
-
-            @pl.when(z > 0)
-            def _():
-                copy(k, me, 2).start()
-
-            copy(k, me, 0).start()
-
-        def step(s, _):
-            for k in range(chunks):
-
-                @pl.when(z - s >= 0)
-                def _():
-                    block = me - 2 * s
-                    landed(k, block)
-
-                    @pl.when(z < Z - 1)
-                    def _():
-                        copy(k, block, 1).start()
-
-                    copy(k, block, 0).start()
-
-                @pl.when(z + s < Z)
-                def _():
-                    block = me + 2 * s
-                    landed(k, block)
-
-                    @pl.when(z > 0)
-                    def _():
-                        copy(k, block, 2).start()
-
-                    copy(k, block, 0).start()
-
-            before = s - 1
-
-            @pl.when(z - before >= 0)
-            def _():
-                for k in range(chunks):
-                    landed(k, partner - 2 * before)
-                process(z - before)
-
-            @pl.when((before > 0) & (z + before < Z))
-            def _():
-                for k in range(chunks):
-                    landed(k, partner + 2 * before)
-                process(z + before)
-
-            return 0
-
-        lax.fori_loop(1, Z + 1, step, 0)
-
-        def drain(s, _):
-            for k in range(chunks):
-
-                @pl.when(z - s >= 0)
-                def _():
-                    block = me - 2 * s
-
-                    @pl.when(z < Z - 1)
-                    def _():
-                        copy(k, block, 1).wait_send()
-
-                    copy(k, block, 0).wait_send()
-
-                    @pl.when((s == 0) & (z > 0))
-                    def _():
-                        copy(k, block, 2).wait_send()
-
-                @pl.when((s > 0) & (z + s < Z))
-                def _():
-                    block = me + 2 * s
-
-                    @pl.when(z > 0)
-                    def _():
-                        copy(k, block, 2).wait_send()
-
-                    copy(k, block, 0).wait_send()
-
-            return 0
-
-        return lambda: lax.fori_loop(0, Z, drain, 0)
-
     heads = q_ref.shape[2]
     span = k_ref.shape[2]
     hd = q_ref.shape[3]
@@ -219,6 +84,8 @@
     live = jnp.stack(
         [jnp.full((heads, span), len_ref[r // rows, r % rows], jnp.int32) for r in range(R)]
     )
+
+    per_chunk = heads // SA
 
     def attend(g):
         scores = lax.dot_general(
@@ -234,18 +101,156 @@
         )
         mixed[...] = result.reshape(R * heads, hd)
         for j in range(heads):
-            att[g, pos(me), :, j * hd : (j + 1) * hd] = mixed[pl.ds(j, R, stride=heads), :].astype(BF16)
+            chunk, column = g * SA + j // per_chunk, j % per_chunk * hd
+            att[chunk, pos(me), :, column : column + hd] = mixed[pl.ds(j, R, stride=heads), :].astype(BF16)
+
+    for g in range(G):
+        attend(g)
+
+    pl.semaphore_wait(barrier, E - 1 + H - 1)
+
+    def share_copy(dst):
+        return pltpu.make_async_remote_copy(
+            src_ref=wbuf.at[pos(me)], dst_ref=wbuf.at[pos(me)],
+            send_sem=sh_send.at[dst], recv_sem=sh_recv.at[me],
+            device_id={"ep": dst}, device_id_type=MESH,
+        )
+
+    def res_copy(dst):
+        return pltpu.make_async_remote_copy(
+            src_ref=res_ref.at[:, pl.ds(pl.multiple_of(dst * CB, CB), CB)], dst_ref=resb.at[me // H],
+            send_sem=rs_send.at[dst], recv_sem=rs_recv.at[me],
+            device_id={"ep": dst}, device_id_type=MESH,
+        )
+
+    def spread(i, _):
+        dst = (me + i) % E
+
+        @pl.when(h == me % H)
+        def _():
+            res_copy(dst).start()
+
+        share_copy(dst).start()
+        return 0
+
+    lax.fori_loop(1, E, spread, 0)
+
+    @pl.when(h == me % H)
+    def _():
+        resb[me // H] = res_ref[:, pl.ds(pl.multiple_of(me * CB, CB), CB)]
+
+    def gather(place, send, recv, chunks, process):
+        def copy(k, block, way):
+            target = (partner, me + 2, me - 2)[way]
+            return pltpu.make_async_remote_copy(
+                src_ref=place(k, block), dst_ref=place(k, block),
+                send_sem=send.at[k, block, way], recv_sem=recv.at[k, block],
+                device_id={"ep": target}, device_id_type=MESH,
+            )
+
+        def landed(k, block):
+            pltpu.make_async_remote_copy(
+                src_ref=place(k, block), dst_ref=place(k, block),
+                send_sem=send.at[k, block, 0], recv_sem=recv.at[k, block],
+                device_id={"ep": partner}, device_id_type=MESH,
+            ).wait_recv()
+
+        for k in range(chunks):
+
+            @pl.when(z < Z - 1)
+            def _():
+                copy(k, me, 1).start()
+
+            @pl.when(z > 0)
+            def _():
+                copy(k, me, 2).start()
+
+            copy(k, me, 0).start()
+
+        def step(s, _):
+            for k in range(chunks):
+
+                @pl.when(z - s >= 0)
+                def _():
+                    block = me - 2 * s
+                    landed(k, block)
+
+                    @pl.when(z < Z - 1)
+                    def _():
+                        copy(k, block, 1).start()
+
+                    copy(k, block, 0).start()
+
+                @pl.when(z + s < Z)
+                def _():
+                    block = me + 2 * s
+                    landed(k, block)
+
+                    @pl.when(z > 0)
+                    def _():
+                        copy(k, block, 2).start()
+
+                    copy(k, block, 0).start()
+
+            before = s - 1
+
+            @pl.when(z - before >= 0)
+            def _():
+                for k in range(chunks):
+                    landed(k, partner - 2 * before)
+                process(z - before)
+
+            @pl.when((before > 0) & (z + before < Z))
+            def _():
+                for k in range(chunks):
+                    landed(k, partner + 2 * before)
+                process(z + before)
+
+            return 0
+
+        lax.fori_loop(1, Z + 1, step, 0)
+
+        def drain(s, _):
+            for k in range(chunks):
+
+                @pl.when(z - s >= 0)
+                def _():
+                    block = me - 2 * s
+
+                    @pl.when(z < Z - 1)
+                    def _():
+                        copy(k, block, 1).wait_send()
+
+                    copy(k, block, 0).wait_send()
+
+                    @pl.when((s == 0) & (z > 0))
+                    def _():
+                        copy(k, block, 2).wait_send()
+
+                @pl.when((s > 0) & (z + s < Z))
+                def _():
+                    block = me + 2 * s
+
+                    @pl.when(z > 0)
+                    def _():
+                        copy(k, block, 2).wait_send()
+
+                    copy(k, block, 0).wait_send()
+
+            return 0
+
+        return lambda: lax.fori_loop(0, Z, drain, 0)
 
     drain_att = gather(
-        lambda k, block: att.at[k, pos(block)], a_send, a_recv, G, attend, lambda chip: None
+        lambda k, block: att.at[k, pos(block)], a_send, a_recv, G * SA, lambda chip: None
     )
 
     loads[3].wait()
-    width = heads * hd
+    width = per_chunk * hd
 
     def project(part):
         total = jnp.zeros((PER * R, CB), F32)
-        for g in range(G):
+        for g in range(G * SA):
             rows_in = att[g, pl.ds(part * PER, PER)].astype(F32).reshape(PER * R, width)
             total = total + jnp.dot(
                 rows_in.astype(BF16), wo[g * width : (g + 1) * width, :],
@@ -253,16 +258,20 @@
             )
         return total.reshape(PER, R, CB)
 
-    def hx_copy(i):
+    def piece_rows(u):
+        return pl.ds(u * (PER // S), PER // S)
+
+    def hx_copy(i, u):
         return pltpu.make_async_remote_copy(
-            src_ref=hx_out.at[i - 1], dst_ref=hx_in.at[i - 1],
-            send_sem=hx_send.at[i - 1], recv_sem=hx_recv.at[i - 1],
+            src_ref=hx_out.at[i - 1, piece_rows(u)], dst_ref=hx_in.at[i - 1, piece_rows(u)],
+            send_sem=hx_send.at[i - 1, u], recv_sem=hx_recv.at[i - 1, u],
             device_id={"hg": (h + i) % H}, device_id_type=MESH,
         )
 
     for i in range(1, H):
         hx_out[i - 1] = project((h + i) % H).astype(BF16)
-        hx_copy(i).start()
+        for u in range(S):
+            hx_copy(i, u).start()
     own_part = project(h)
 
     def landed_at(ref, place, sem):
@@ -284,10 +293,14 @@
 
     lax.fori_loop(1, E, spread_landed, 0)
     own_part = own_part + resb[...].astype(F32)
-    for i in range(1, H):
-        hx_copy(i).wait_recv()
-        own_part = own_part + hx_in[i - 1].astype(F32)
-    hid[me, h] = own_part.astype(BF16)
+
+    def hidden_piece(u):
+        first, last = u * (PER // S), (u + 1) * (PER // S)
+        value = own_part[first:last]
+        for i in range(1, H):
+            hx_copy(i, u).wait_recv()
+            value = value + hx_in[i - 1, first:last].astype(F32)
+        hid[me, h, first:last] = value.astype(BF16)
 
     acc_g[...] = jnp.zeros_like(acc_g)
     acc_u[...] = jnp.zeros_like(acc_u)
@@ -309,39 +322,42 @@
 
         lax.fori_loop(0, 2, piece, 0)
 
-    def hid_copy(block, part, way):
+    def hid_copy(block, part, way, u):
         if way < 3:
             device = {"ep": (partner, me + 2, me - 2)[way]}
         else:
             device = {"hg": (h + way - 2) % H}
         return pltpu.make_async_remote_copy(
-            src_ref=hid.at[block, part], dst_ref=hid.at[block, part],
-            send_sem=h_send.at[block, part, way], recv_sem=h_recv.at[block, part],
+            src_ref=hid.at[block, part, piece_rows(u)],
+            dst_ref=hid.at[block, part, piece_rows(u)],
+            send_sem=h_send.at[block, part, u * (H + 2) + way],
+            recv_sem=h_recv.at[block, part, u],
             device_id=device, device_id_type=MESH,
         )
 
-    def hid_pass(block, go, right, left):
+    def hid_pass(block, u, go, right, left):
         for way, wanted in ((1, right), (2, left)):
             if wanted is not False:
 
                 @pl.when(wanted)
                 def _():
-                    go(hid_copy(block, h, way))
+                    go(hid_copy(block, h, way, u))
 
         for i in range(1, H):
-            go(hid_copy(block, h, 2 + i))
-        go(hid_copy(block, h, 0))
-
-    def hid_cross(block, go, wait):
+            go(hid_copy(block, h, 2 + i, u))
+        go(hid_copy(block, h, 0, u))
+
+    def hid_cross(block, u, go, wait):
         for i in range(1, H):
             part = (h + i) % H
             if wait:
-                hid_copy(block, part, 0).wait_recv()
-            go(hid_copy(block, part, 0))
+                hid_copy(block, part, 0, u).wait_recv()
+            go(hid_copy(block, part, 0, u))
 
     def hid_take(chip):
         for part in range(H):
-            hid_copy(chip * 2 + (1 - c), part, 0).wait_recv()
+            for u in range(S):
+                hid_copy(chip * 2 + (1 - c), part, 0, u).wait_recv()
         experts_in(chip)
 
     def sides(s, action):
@@ -359,35 +375,47 @@
     def sent(copy):
         copy.wait_send()
 
-    hid_pass(me, start, z < Z - 1, z > 0)
+    for u in range(S):
+        hidden_piece(u)
+        hid_pass(me, u, start, z < Z - 1, z > 0)
 
     def hid_step(s, _):
-        def forward(chip, from_left):
-            block = chip * 2 + c
-            hid_copy(block, h, 0).wait_recv()
-            hid_pass(block, start, (z < Z - 1) if from_left else False, False if from_left else (z > 0))
-
-        sides(s, forward)
-        sides(s - 1, lambda chip, from_left: hid_cross(chip * 2 + c, start, True))
+        for u in range(S):
+
+            def forward(chip, from_left):
+                block = chip * 2 + c
+                hid_copy(block, h, 0, u).wait_recv()
+                hid_pass(
+                    block, u, start,
+                    (z < Z - 1) if from_left else False, False if from_left else (z > 0),
+                )
+
+            sides(s, forward)
+        for u in range(S):
+            sides(s - 1, lambda chip, from_left: hid_cross(chip * 2 + c, u, start, True))
         sides(s - 2, lambda chip, from_left: hid_take(chip))
         return 0
 
     lax.fori_loop(1, Z + 2, hid_step, 0)
 
     def drain_hid():
-        hid_pass(me, sent, z < Z - 1, z > 0)
+        for u in range(S):
+            hid_pass(me, u, sent, z < Z - 1, z > 0)
 
         def drain(s, _):
-            def passed(chip, from_left):
-                hid_pass(
-                    chip * 2 + c, sent, (z < Z - 1) if from_left else False, False if from_left else (z > 0)
-                )
-
-            @pl.when(s > 0)
-            def _():
-                sides(s, passed)
-
-            sides(s, lambda chip, from_left: hid_cross(chip * 2 + c, sent, False))
+            for u in range(S):
+
+                def passed(chip, from_left):
+                    hid_pass(
+                        chip * 2 + c, u, sent,
+                        (z < Z - 1) if from_left else False, False if from_left else (z > 0),
+                    )
+
+                @pl.when(s > 0)
+                def _():
+                    sides(s, passed)
+
+                sides(s, lambda chip, from_left: hid_cross(chip * 2 + c, u, sent, False))
             return 0
 
         lax.fori_loop(0, Z, drain, 0)
@@ -479,8 +507,10 @@
             total = total + d3_in[i - 1, q].astype(F32)
         for i in range(QW // part_width):
             column = i * part_width
-            p = (h * DH + q * QW + column) // CB
-            part = hid[p, me % H, me // H].astype(F32) + total[:, column : column + part_width]
+            p = h * (DH // CB) + (q * QW + column) // CB
+            inside = (q * QW + column) % CB
+            part = hid[p, me % H, me // H, :, inside : inside + part_width].astype(F32)
+            part = part + total[:, column : column + part_width]
             out_ref[:, q * QW + column : q * QW + column + part_width] = part.astype(BF16)
 
     drain_att()
@@ -498,7 +528,8 @@
 
     lax.fori_loop(1, E, spread_done, 0)
     for i in range(1, H):
-        hx_copy(i).wait_send()
+        for u in range(S):
+            hx_copy(i, u).wait_send()
     for q in range(Q):
         for i in range(H):
             d1_copy(i, q).wait_send()
@@ -531,7 +562,7 @@
     J, _, hid_local = gate_weight.shape
     CB = D // E
     DH = D // H
-    Q = max(1, DH // 512)
+    Q = max(1, DH // 256)
     QW = DH // Q
     PER = E // H
     packed = J * E * 8 == 128 and R % 8 == 0
@@ -539,7 +570,9 @@
     ROWS = E * R
     share_rows = R // 8 if packed else R
     width = heads // G * hd
-    dims = (E, H, G, R, Q, QW, J, packed)
+    SA = 2 if heads // G % 2 == 0 else 1
+    S = 2 if PER % 2 == 0 else 1
+    dims = (E, H, G, R, Q, QW, J, packed, SA, S)
     vmem = pl.BlockSpec(memory_space=pltpu.VMEM)
     hbm = pl.BlockSpec(memory_space=pl.ANY)
     dma = pltpu.SemaphoreType.DMA
@@ -557,7 +590,7 @@
             pltpu.VMEM(up_weight.shape, BF16),
             pltpu.VMEM(down_weight.shape, BF16),
             pltpu.VMEM((R * (heads // G), hd), F32),
-            pltpu.VMEM((G, E, R, width), BF16),
+            pltpu.VMEM((G * SA, E, R, width // SA), BF16),
             pltpu.VMEM((PER, R, CB), BF16),
             pltpu.VMEM((E, share_rows, 128), F32),
             pltpu.VMEM((H - 1, PER, R, CB), BF16),
@@ -576,9 +609,9 @@
             pltpu.VMEM((Z - 1, Q, R, QW), BF16),
             dma((7,)),
             dma((E,)), dma((E,)), dma((E,)), dma((E,)),
-            dma((G, E, 3)), dma((G, E)),
-            dma((H - 1,)), dma((H - 1,)),
-            dma((E, H, H + 2)), dma((E, H)),
+            dma((G * SA, E, 3)), dma((G * SA, E)),
+            dma((H - 1, S)), dma((H - 1, S)),
+            dma((E, H, S * (H + 2))), dma((E, H, S)),
             dma((H, Q)), dma((H, Q)),
             dma((H - 1, Q)), dma((H - 1, Q)),
             dma((Z - 1, Q)), dma((Z - 1, Q)),

time: 67.3 us -> 67.8 us (level)
  no operation moved by 1% of the time
where the time goes in v3:
time: 67.8 us; the launch traced here: 67.7 us
  Pallas kernels  66.1 us (97%)
  local copies, waits for them, and re-layouts  1.54 us (2%)
    pallas_call x1, Pallas kernels, shards(): pl.pallas_call(functools.partial(layer_kernel, dims), out_shape=jax.Shape...  66.1 us
    unnamed x1, local copies, waits for them, and re-layouts  1.54 us

profile of v3, /device:TPU:0, one launch (start us, length us, event | category | flops | bytes accessed | tf_op | source)
XLA Modules:
  0.0 67.7 jit_solution(11902057382717941068)
XLA Ops:
  0.0 66.1 %layer.1 = bf16[24,2048]{1,0:T(8,128)(2,1)} custom-call(s32[3,8]{1,0:T(4,128)} %len_ref.1, bf16[24,4096]{1,0:T(8,128)(2,1)} %bitcast.11, f32[1,4096]{1,0:T(1,128)} %bitcast.13, s32[24,8]{1,0:T(8,128)} %bitcast.14, f32[24,8]{1,0:T(8,128)} %bitcast.15, bf16[24,2,16,128]{3,2,1,0:T(8,128)(2,1)} %bitcast.12, bf16[24,2,96,128]{3,2,1,0:T(8,128)(2,1)} %bitcast.8, ...), custom_call_target="tpu_custom_call" | custom-call | tf_op jit(solution)/shard_map/layer/pallas_call | solution.py:579
  66.1 1.5 %copy.14 = bf16[3,8,2048]{2,1,0:T(8,128)(2,1)} copy(bf16[3,8,2048]{2,1,0:T(8,128)(2,1)} %bitcast.10) | data formatting | bytes 196608

commit v4 on v3

--- a/solution.py
+++ b/solution.py
@@ -478,15 +478,19 @@
         d1_copy(i, q).start()
         mine[i, q] = jnp.where(c == 0, first, second)
 
-    for q in range(Q):
-        for i in range(1, H):
-            down(i, q)
-    for q in range(Q):
-        down(0, q)
+    def cross(q):
         for i in range(1, H):
             d1_copy(i, q).wait_recv()
             d2_out[i - 1, q] = (mine[i, q] + d1_in[i, q].astype(F32)).astype(BF16)
             d2_copy(i, q).start()
+
+    for q in range(Q):
+        for i in range(1, H):
+            down(i, q)
+        down(0, q)
+        if q > 0:
+            cross(q - 1)
+    cross(Q - 1)
 
     for q in range(Q):
         d1_copy(0, q).wait_recv()
@@ -562,7 +566,7 @@
     J, _, hid_local = gate_weight.shape
     CB = D // E
     DH = D // H
-    Q = max(1, DH // 256)
+    Q = max(1, DH // 512)
     QW = DH // Q
     PER = E // H
     packed = J * E * 8 == 128 and R % 8 == 0

time: 67.8 us -> 66.1 us (0.975)
  Pallas kernels: 66.1 us -> 64.4 us
    pallas_call x1, Pallas kernels: 66.1 us -> 64.4 us  [shards(): pl.pallas_call(functools.partial(layer_kernel, dims), out_shape=jax.Shape...]
where the time goes in v4:
time: 66.1 us; the launch traced here: 65.9 us
  Pallas kernels  64.4 us (97%)
  local copies, waits for them, and re-layouts  1.54 us (2%)
    pallas_call x1, Pallas kernels, shards(): pl.pallas_call(functools.partial(layer_kernel, dims), out_shape=jax.Shape...  64.4 us
    unnamed x1, local copies, waits for them, and re-layouts  1.54 us

profile of v4, /device:TPU:0, one launch (start us, length us, event | category | flops | bytes accessed | tf_op | source)
XLA Modules:
  0.0 65.9 jit_solution(17388536932992704666)
XLA Ops:
  0.0 64.4 %layer.1 = bf16[24,2048]{1,0:T(8,128)(2,1)} custom-call(s32[3,8]{1,0:T(4,128)} %len_ref.1, bf16[24,4096]{1,0:T(8,128)(2,1)} %bitcast.11, f32[1,4096]{1,0:T(1,128)} %bitcast.13, s32[24,8]{1,0:T(8,128)} %bitcast.14, f32[24,8]{1,0:T(8,128)} %bitcast.15, bf16[24,2,16,128]{3,2,1,0:T(8,128)(2,1)} %bitcast.12, bf16[24,2,96,128]{3,2,1,0:T(8,128)(2,1)} %bitcast.8, ...), custom_call_target="tpu_custom_call" | custom-call | tf_op jit(solution)/shard_map/layer/pallas_call | solution.py:583
  64.4 1.5 %copy.14 = bf16[3,8,2048]{2,1,0:T(8,128)(2,1)} copy(bf16[3,8,2048]{2,1,0:T(8,128)(2,1)} %bitcast.10) | data formatting | bytes 196608
